TPU v7x, 32 devices: a whole 2x2x4 slice. The times are simulated.
32 devices in a mesh: dp: 8 (over z, y), fsdp: 4 (over x, core).
Axes of the slice: x: 2, y: 2, z: 4, core: 2. Of those that a mesh axis runs over, the one named last changes fastest.
Arguments:
- latents: bfloat16 [32, 864, 768], P(('dp', 'fsdp')), may hold values from -6 to 6
- text_rows: bfloat16 [32, 256, 768], P(('dp', 'fsdp')), may hold values from -6 to 6
- out_grad: bfloat16 [32, 864, 768], P(('dp', 'fsdp')), as said below
- frame_len: int32 [32], P(('dp', 'fsdp')), may hold values from 86 to 860, as said below
- text_len: int32 [32], P(('dp', 'fsdp')), may hold values from 77 to 256, as said below
- timestep: int32 [32], P(('dp', 'fsdp')), may hold values from 0 to 999
- w_ada: bfloat16 [768, 6912], P('dp', 'fsdp'), may hold values from -0.625 to 0.625
- w_qkv: bfloat16 [768, 2304], P('dp', 'fsdp'), may hold values from -0.21875 to 0.21875
- w_out: bfloat16 [768, 768], P('dp', 'fsdp'), may hold values from -0.625 to 0.625
- w_cq: bfloat16 [768, 768], P('dp', 'fsdp'), may hold values from -0.21875 to 0.21875
- w_ckv: bfloat16 [768, 1536], P('dp', 'fsdp'), may hold values from -0.21875 to 0.21875
- w_cout: bfloat16 [768, 768], P('dp', 'fsdp'), may hold values from -0.625 to 0.625
- w_fc1: bfloat16 [768, 3072], P('dp', 'fsdp'), may hold values from -0.21875 to 0.21875
- w_fc2: bfloat16 [3072, 768], P('dp', 'fsdp'), may hold values from -0.109375 to 0.109375
Outputs:
- layer_out: float32 [32, 864, 768], P(('dp', 'fsdp'))
- latent_grad: float32 [32, 864, 768], P(('dp', 'fsdp'))
- text_grad: float32 [32, 256, 768], P(('dp', 'fsdp'))
- grad_ada: float32 [768, 6912], P('dp', 'fsdp')
- grad_qkv: float32 [768, 2304], P('dp', 'fsdp')
- grad_out: float32 [768, 768], P('dp', 'fsdp')
- grad_cq: float32 [768, 768], P('dp', 'fsdp')
- grad_ckv: float32 [768, 1536], P('dp', 'fsdp')
- grad_cout: float32 [768, 768], P('dp', 'fsdp')
- grad_fc1: float32 [768, 3072], P('dp', 'fsdp')
- grad_fc2: float32 [3072, 768], P('dp', 'fsdp')
Inputs may be any that keep to these rules, and one draw needn't show every extreme that they name: A clip's frames fill slots 0 to frame_len - 1; some clip has exactly 860 frames. A clip's text rows fill slots 0 to text_len - 1; some clip uses all 256 slots. out_grad is exactly zero at every slot >= frame_len of its clip.
All inputs are finite; a program needn't handle non-finite values.
Results may differ from a plain program's by a relative error of at most 0.034.
Values may be sent and summed in bfloat16 or wider, within the bound.
A program may use at most 192 MiB of HBM per device.

v0:
```python
import math

import jax
import jax.numpy as jnp
from jax import lax
from jax.sharding import PartitionSpec as P

HEADS = 12


norm_eps = 1e-06


def sinusoid(time_value, model_width):
    half_width = model_width // 2
    frequency = jnp.exp(-math.log(10000.0) * jnp.arange(half_width, dtype=jnp.float32) / half_width)
    angles = time_value.astype(jnp.float32) * frequency
    return jnp.concatenate([jnp.cos(angles), jnp.sin(angles)], axis=-1)


def normalize(values):
    center = values - jnp.mean(values, -1, keepdims=True)
    spread = jnp.mean(center * center, -1, keepdims=True)
    inverse = lax.rsqrt(spread + norm_eps)
    return (center * inverse, inverse)


def norm_back(upstream, normed, inverse, scale_row):
    dshift = jnp.sum(upstream, 0)
    dscale = jnp.sum(upstream * normed, 0)
    scaled = upstream * (1.0 + scale_row)
    centered = (
        scaled
        - jnp.mean(scaled, -1, keepdims=True)
        - normed * jnp.mean(scaled * normed, -1, keepdims=True)
    )
    return (inverse * centered, dshift, dscale)


def outer_sum(left, right):
    return lax.dot_general(
        left, right, (((0,), (0,)), ((), ())), preferred_element_type=jnp.float32
    )


def through(gradient, matrix):
    return lax.dot_general(
        gradient, matrix, (((1,), (1,)), ((), ())), preferred_element_type=jnp.float32
    )


def gelu_tanh(values):
    return jax.nn.gelu(values, approximate=True)


def group_count(head_count):
    return head_count // 4


def split_groups(array, groups):
    rows, head_count, head_size = array.shape
    return jnp.moveaxis(array.reshape(rows, groups, head_count // groups, head_size), 1, 0)


def join_groups(array):
    return jnp.moveaxis(array, 0, 1).reshape(array.shape[1], -1)


def attend_forward(query_rows, key_rows, value_rows, key_valid):
    factor = query_rows.shape[-1] ** (-0.5)
    groups = group_count(query_rows.shape[1])

    def one_group(packed):
        query_part, key_part, value_part = packed
        scores = (
            jnp.einsum("shd,thd->hst", query_part, key_part, preferred_element_type=jnp.float32)
            * factor
        )
        scores = jnp.where(key_valid[None, None, :], scores, -1e30)
        largest = jnp.max(scores, -1, keepdims=True)
        exponent = jnp.exp(scores - largest)
        summed = jnp.sum(exponent, -1, keepdims=True)
        shares = (exponent / summed).astype(jnp.bfloat16)
        mixed_part = jnp.einsum(
            "hst,thd->shd", shares, value_part, preferred_element_type=jnp.float32
        )
        return (mixed_part.astype(jnp.bfloat16), (largest + jnp.log(summed))[..., 0])

    mixed_heads, log_total = lax.map(
        one_group,
        (
            split_groups(query_rows, groups),
            split_groups(key_rows, groups),
            split_groups(value_rows, groups),
        ),
    )
    return (join_groups(mixed_heads), log_total)


def attend_back(query_rows, key_rows, value_rows, key_valid, log_total, upstream):
    factor = query_rows.shape[-1] ** (-0.5)
    groups = group_count(query_rows.shape[1])
    upstream_heads = upstream.reshape(query_rows.shape)

    def one_group(packed):
        query_part, key_part, value_part, log_part, upstream_part = packed
        scores = (
            jnp.einsum("shd,thd->hst", query_part, key_part, preferred_element_type=jnp.float32)
            * factor
        )
        scores = jnp.where(key_valid[None, None, :], scores, -1e30)
        shares = jnp.exp(scores - log_part[..., None])
        share_grad = jnp.einsum(
            "shd,thd->hst", upstream_part, value_part, preferred_element_type=jnp.float32
        )
        score_grad = (
            shares * (share_grad - jnp.sum(shares * share_grad, -1, keepdims=True))
        ).astype(jnp.bfloat16)
        query_grad = (
            jnp.einsum("hst,thd->shd", score_grad, key_part, preferred_element_type=jnp.float32)
            * factor
        )
        key_grad = (
            jnp.einsum("hst,shd->thd", score_grad, query_part, preferred_element_type=jnp.float32)
            * factor
        )
        value_grad = jnp.einsum(
            "hst,shd->thd",
            shares.astype(jnp.bfloat16),
            upstream_part,
            preferred_element_type=jnp.float32,
        )
        return (query_grad, key_grad, value_grad)

    query_grad, key_grad, value_grad = lax.map(
        one_group,
        (
            split_groups(query_rows, groups),
            split_groups(key_rows, groups),
            split_groups(value_rows, groups),
            log_total,
            split_groups(upstream_heads, groups),
        ),
    )
    return (join_groups(query_grad), join_groups(key_grad), join_groups(value_grad))


def body(
    latents,
    text_rows,
    out_grad,
    frame_len,
    text_len,
    timestep,
    w_ada,
    w_qkv,
    w_out,
    w_cq,
    w_ckv,
    w_cout,
    w_fc1,
    w_fc2,
):
    columns = (
        lax.all_gather(w_ada, "fsdp", axis=1, tiled=True),
        lax.all_gather(w_qkv, "fsdp", axis=1, tiled=True),
        lax.all_gather(w_out, "fsdp", axis=1, tiled=True),
        lax.all_gather(w_cq, "fsdp", axis=1, tiled=True),
        lax.all_gather(w_ckv, "fsdp", axis=1, tiled=True),
        lax.all_gather(w_cout, "fsdp", axis=1, tiled=True),
        lax.all_gather(w_fc1, "fsdp", axis=1, tiled=True),
        lax.all_gather(w_fc2, "fsdp", axis=1, tiled=True),
    )
    weights = (
        lax.all_gather(columns[0], "dp", axis=0, tiled=True),
        lax.all_gather(columns[1], "dp", axis=0, tiled=True),
        lax.all_gather(columns[2], "dp", axis=0, tiled=True),
        lax.all_gather(columns[3], "dp", axis=0, tiled=True),
        lax.all_gather(columns[4], "dp", axis=0, tiled=True),
        lax.all_gather(columns[5], "dp", axis=0, tiled=True),
        lax.all_gather(columns[6], "dp", axis=0, tiled=True),
        lax.all_gather(columns[7], "dp", axis=0, tiled=True),
    )
    full_ada, full_qkv, full_out, full_cq, full_ckv, full_cout, full_fc1, full_fc2 = weights
    latent = latents[0].astype(jnp.float32)
    text_block = text_rows[0]
    slot_count = latent.shape[0]
    model_width = latent.shape[1]
    text_slots = text_block.shape[0]
    head_size = model_width // HEADS
    frame_valid = jnp.arange(slot_count) < frame_len[0]
    text_valid = jnp.arange(text_slots) < text_len[0]
    condition = jax.nn.silu(sinusoid(timestep[0], model_width)).astype(jnp.bfloat16)
    modulation = jnp.dot(condition[None, :], full_ada, preferred_element_type=jnp.float32).reshape(
        9, model_width
    )
    normed_one, inverse_one = normalize(latent)
    hidden_one = (normed_one * (1.0 + modulation[1]) + modulation[0]).astype(jnp.bfloat16)
    packed = jnp.dot(hidden_one, full_qkv, preferred_element_type=jnp.float32).astype(jnp.bfloat16)
    packed = packed.reshape(slot_count, 3, HEADS, head_size)
    mixed_one, log_one = attend_forward(packed[:, 0], packed[:, 1], packed[:, 2], frame_valid)
    branch_one = jnp.dot(mixed_one, full_out, preferred_element_type=jnp.float32)
    after_self = latent + modulation[2] * branch_one
    normed_two, inverse_two = normalize(after_self)
    hidden_two = (normed_two * (1.0 + modulation[4]) + modulation[3]).astype(jnp.bfloat16)
    query_two = jnp.dot(hidden_two, full_cq, preferred_element_type=jnp.float32).astype(
        jnp.bfloat16
    )
    query_two = query_two.reshape(slot_count, HEADS, head_size)
    memory = jnp.dot(text_block, full_ckv, preferred_element_type=jnp.float32).astype(jnp.bfloat16)
    memory = memory.reshape(text_slots, 2, HEADS, head_size)
    mixed_two, log_two = attend_forward(query_two, memory[:, 0], memory[:, 1], text_valid)
    branch_two = jnp.dot(mixed_two, full_cout, preferred_element_type=jnp.float32)
    after_cross = after_self + modulation[5] * branch_two
    normed_three, inverse_three = normalize(after_cross)
    hidden_three = (normed_three * (1.0 + modulation[7]) + modulation[6]).astype(jnp.bfloat16)
    pre_gelu = jnp.dot(hidden_three, full_fc1, preferred_element_type=jnp.float32)
    activated = gelu_tanh(pre_gelu).astype(jnp.bfloat16)
    branch_three = jnp.dot(activated, full_fc2, preferred_element_type=jnp.float32)
    layer_out = after_cross + modulation[8] * branch_three
    columns = (
        lax.all_gather(w_ada, "fsdp", axis=1, tiled=True),
        lax.all_gather(w_qkv, "fsdp", axis=1, tiled=True),
        lax.all_gather(w_out, "fsdp", axis=1, tiled=True),
        lax.all_gather(w_cq, "fsdp", axis=1, tiled=True),
        lax.all_gather(w_ckv, "fsdp", axis=1, tiled=True),
        lax.all_gather(w_cout, "fsdp", axis=1, tiled=True),
        lax.all_gather(w_fc1, "fsdp", axis=1, tiled=True),
        lax.all_gather(w_fc2, "fsdp", axis=1, tiled=True),
    )
    weights = (
        lax.all_gather(columns[0], "dp", axis=0, tiled=True),
        lax.all_gather(columns[1], "dp", axis=0, tiled=True),
        lax.all_gather(columns[2], "dp", axis=0, tiled=True),
        lax.all_gather(columns[3], "dp", axis=0, tiled=True),
        lax.all_gather(columns[4], "dp", axis=0, tiled=True),
        lax.all_gather(columns[5], "dp", axis=0, tiled=True),
        lax.all_gather(columns[6], "dp", axis=0, tiled=True),
        lax.all_gather(columns[7], "dp", axis=0, tiled=True),
    )
    full_ada, full_qkv, full_out, full_cq, full_ckv, full_cout, full_fc1, full_fc2 = weights
    upstream = out_grad[0].astype(jnp.float32)
    dbranch_three = (modulation[8] * upstream).astype(jnp.bfloat16)
    dgate_three = jnp.sum(upstream * branch_three, 0)
    grad_fc2 = outer_sum(activated, dbranch_three)
    dactivated = through(dbranch_three, full_fc2)
    gelu_value, gelu_pull = jax.vjp(gelu_tanh, pre_gelu)
    dinner = gelu_pull(dactivated)[0].astype(jnp.bfloat16)
    grad_fc1 = outer_sum(hidden_three, dinner)
    back_three, dshift_three, dscale_three = norm_back(
        through(dinner, full_fc1), normed_three, inverse_three, modulation[7]
    )
    dcross = upstream + back_three
    dbranch_two = (modulation[5] * dcross).astype(jnp.bfloat16)
    dgate_two = jnp.sum(dcross * branch_two, 0)
    grad_cout = outer_sum(mixed_two, dbranch_two)
    dmixed_two = through(dbranch_two, full_cout).astype(jnp.bfloat16)
    dquery_two, dkeys_two, dvalues_two = attend_back(
        query_two, memory[:, 0], memory[:, 1], text_valid, log_two, dmixed_two
    )
    dquery_flat = dquery_two.astype(jnp.bfloat16)
    dmemory = jnp.concatenate([dkeys_two, dvalues_two], -1).astype(jnp.bfloat16)
    grad_cq = outer_sum(hidden_two, dquery_flat)
    grad_ckv = outer_sum(text_block, dmemory)
    text_grad = through(dmemory, full_ckv)
    back_two, dshift_two, dscale_two = norm_back(
        through(dquery_flat, full_cq), normed_two, inverse_two, modulation[4]
    )
    grad_self = dcross + back_two
    dbranch_one = (modulation[2] * grad_self).astype(jnp.bfloat16)
    dgate_one = jnp.sum(grad_self * branch_one, 0)
    grad_out = outer_sum(mixed_one, dbranch_one)
    dmixed_one = through(dbranch_one, full_out).astype(jnp.bfloat16)
    dquery_one, dkeys_one, dvalues_one = attend_back(
        packed[:, 0], packed[:, 1], packed[:, 2], frame_valid, log_one, dmixed_one
    )
    dpacked = jnp.concatenate([dquery_one, dkeys_one, dvalues_one], -1).astype(jnp.bfloat16)
    grad_qkv = outer_sum(hidden_one, dpacked)
    back_one, dshift_one, dscale_one = norm_back(
        through(dpacked, full_qkv), normed_one, inverse_one, modulation[1]
    )
    latent_grad = grad_self + back_one
    dmodulation = (
        jnp.stack(
            [
                dshift_one,
                dscale_one,
                dgate_one,
                dshift_two,
                dscale_two,
                dgate_two,
                dshift_three,
                dscale_three,
                dgate_three,
            ]
        )
        .reshape(1, -1)
        .astype(jnp.bfloat16)
    )
    grad_ada = outer_sum(condition[None, :], dmodulation)
    reduced = (
        lax.psum_scatter(
            grad_ada.astype(jnp.bfloat16), "dp", scatter_dimension=0, tiled=True
        ).astype(jnp.float32),
        lax.psum_scatter(
            grad_qkv.astype(jnp.bfloat16), "dp", scatter_dimension=0, tiled=True
        ).astype(jnp.float32),
        lax.psum_scatter(
            grad_out.astype(jnp.bfloat16), "dp", scatter_dimension=0, tiled=True
        ).astype(jnp.float32),
        lax.psum_scatter(
            grad_cq.astype(jnp.bfloat16), "dp", scatter_dimension=0, tiled=True
        ).astype(jnp.float32),
        lax.psum_scatter(
            grad_ckv.astype(jnp.bfloat16), "dp", scatter_dimension=0, tiled=True
        ).astype(jnp.float32),
        lax.psum_scatter(
            grad_cout.astype(jnp.bfloat16), "dp", scatter_dimension=0, tiled=True
        ).astype(jnp.float32),
        lax.psum_scatter(
            grad_fc1.astype(jnp.bfloat16), "dp", scatter_dimension=0, tiled=True
        ).astype(jnp.float32),
        lax.psum_scatter(
            grad_fc2.astype(jnp.bfloat16), "dp", scatter_dimension=0, tiled=True
        ).astype(jnp.float32),
    )
    owned_grads = (
        lax.psum_scatter(
            reduced[0].astype(jnp.bfloat16), "fsdp", scatter_dimension=1, tiled=True
        ).astype(jnp.float32),
        lax.psum_scatter(
            reduced[1].astype(jnp.bfloat16), "fsdp", scatter_dimension=1, tiled=True
        ).astype(jnp.float32),
        lax.psum_scatter(
            reduced[2].astype(jnp.bfloat16), "fsdp", scatter_dimension=1, tiled=True
        ).astype(jnp.float32),
        lax.psum_scatter(
            reduced[3].astype(jnp.bfloat16), "fsdp", scatter_dimension=1, tiled=True
        ).astype(jnp.float32),
        lax.psum_scatter(
            reduced[4].astype(jnp.bfloat16), "fsdp", scatter_dimension=1, tiled=True
        ).astype(jnp.float32),
        lax.psum_scatter(
            reduced[5].astype(jnp.bfloat16), "fsdp", scatter_dimension=1, tiled=True
        ).astype(jnp.float32),
        lax.psum_scatter(
            reduced[6].astype(jnp.bfloat16), "fsdp", scatter_dimension=1, tiled=True
        ).astype(jnp.float32),
        lax.psum_scatter(
            reduced[7].astype(jnp.bfloat16), "fsdp", scatter_dimension=1, tiled=True
        ).astype(jnp.float32),
    )
    return (
        layer_out[None],
        latent_grad[None],
        text_grad[None],
        owned_grads[0],
        owned_grads[1],
        owned_grads[2],
        owned_grads[3],
        owned_grads[4],
        owned_grads[5],
        owned_grads[6],
        owned_grads[7],
    )


def solution(mesh):
    placed = (
        P(("dp", "fsdp"), None, None),
        P(("dp", "fsdp"), None, None),
        P(("dp", "fsdp"), None, None),
        P(("dp", "fsdp")),
        P(("dp", "fsdp")),
        P(("dp", "fsdp")),
        P("dp", "fsdp"),
        P("dp", "fsdp"),
        P("dp", "fsdp"),
        P("dp", "fsdp"),
        P("dp", "fsdp"),
        P("dp", "fsdp"),
        P("dp", "fsdp"),
        P("dp", "fsdp"),
    )
    return jax.shard_map(
        body,
        mesh=mesh,
        in_specs=placed,
        out_specs=(
            P(("dp", "fsdp"), None, None),
            P(("dp", "fsdp"), None, None),
            P(("dp", "fsdp"), None, None),
            P("dp", "fsdp"),
            P("dp", "fsdp"),
            P("dp", "fsdp"),
            P("dp", "fsdp"),
            P("dp", "fsdp"),
            P("dp", "fsdp"),
            P("dp", "fsdp"),
            P("dp", "fsdp"),
        ),
        check_vma=False,
    )
```

profile of v0, /device:TPU:0, one launch (start us, length us, event | category | flops | bytes accessed | tf_op | source)
XLA Modules:
  0.0 1568.3 jit_solution(9549854063937385612)
XLA Ops:
  8.0 9.0 all_gather.68
  17.0 13.8 all-gather.28.cloned.1.call-done
  35.4 7.1 all-gather.1
  44.1 5.7 all_gather.66
  50.9 5.6 all_gather.70
  57.5 5.6 all_gather.72
  64.0 8.1 all_gather.74
  72.2 8.1 all_gather.76
  88.9 150.1 %all-gather.12.cloned.1.call-done = bf16[768,6912]{1,0:T(8,128)(2,1)} async-done(((bf16[96,6912]{1,0:T(8,128)(2,1)}), bf16[768,6912]{1,0:T(8,128)(2,1)}) %all-gather.12.cloned.1.call-update) | async-done | bytes 10616848 | tf_op jit(solution)/shard_map/all_gather | solution.py:175
  245.1 59.8 %all-gather.14.cloned.1.call-done = bf16[768,2304]{1,0:T(8,128)(2,1)} async-done(((bf16[96,2304]{1,0:T(8,128)(2,1)}), bf16[768,2304]{1,0:T(8,128)(2,1)}) %all-gather.14.cloned.1.call-update) | async-done | bytes 3538960 | tf_op jit(solution)/shard_map/all_gather | solution.py:176
  305.0 7.4 convolution_convert_fusion
  312.4 6.4 copy.74
  323.8 35.1 %while.56 = (s32[]{:T(128)}, bf16[3,864,4,64]{1,3,2,0:T(8,128)(2,1)}, f32[3,4,864]{2,1,0:T(4,128)S(1)}, bf16[3,864,4,64]{1,3,2,0:T(8,128)(2,1)}, bf16[3,864,4,64...) while((s32[]{:T(128)}, ...), condition=%wide.region_5.6_spmd.clone, body=%wide.region_2.5_spmd.clone.sunk | while | flops 800462336 | bytes 37784708 | solution.py:89
  365.8 23.8 %all-gather.20.cloned.1.call-done = bf16[768,768]{1,0:T(8,128)(2,1)} async-done(((bf16[96,768]{1,0:T(8,128)(2,1)}), bf16[768,768]{1,0:T(8,128)(2,1)}) %all-gather.20.cloned.1.call-update) | async-done | bytes 1179664 | tf_op jit(solution)/shard_map/all_gather | solution.py:178
  397.2 20.1 %while.57 = (s32[]{:T(128)}, bf16[3,864,4,64]{1,3,2,0:T(8,128)(2,1)}, f32[3,4,864]{2,1,0:T(4,128)S(1)}, bf16[3,256,4,64]{1,3,2,0:T(8,128)(2,1)}, bf16[3,864,4,64...) while((s32[]{:T(128)}, ...), condition=%wide.region_11.12_spmd.clone, body=%wide.region_8.11_spmd.clone.sunk | while | flops 237327232 | bytes 11912037 | solution.py:89
  417.3 14.9 all-gather.22.cloned.1.call-done
  438.8 74.3 %all-gather.24.cloned.1.call-done = bf16[768,3072]{1,0:T(8,128)(2,1)} async-done(((bf16[96,3072]{1,0:T(8,128)(2,1)}), bf16[768,3072]{1,0:T(8,128)(2,1)}) %all-gather.24.cloned.1.call-update) | async-done | bytes 4718608 | tf_op jit(solution)/shard_map/all_gather | solution.py:181
  513.1 11.5 fusion.154
  524.6 69.7 %all-gather.26.cloned.1.call-done = bf16[3072,768]{0,1:T(8,128)(2,1)} async-done(((bf16[384,768]{0,1:T(8,128)(2,1)}), bf16[3072,768]{0,1:T(8,128)(2,1)}) %all-gather.26.cloned.1.call-update) | async-done | bytes 4718608 | tf_op jit(solution)/shard_map/all_gather | solution.py:182
  594.4 13.6 fusion.117
  608.0 6.7 multiply_reduce_fusion.2
  614.7 13.9 fusion.137
  640.9 27.6 %while.58 = (s32[]{:T(128)}, bf16[3,864,4,64]{1,3,2,0:T(8,128)(2,1)}, bf16[3,256,4,64]{1,3,2,0:T(8,128)(2,1)}, bf16[3,256,4,64]{1,3,2,0:T(8,128)(2,1)}, bf16[3,2...) while((s32[]{:T(128)}, ...), condition=%wide.region_18.19_spmd.clone, body=%wide.region_16.18_spmd.clone.sunk | while | flops 574477184 | bytes 52504640 | solution.py:135
  695.3 80.5 %while.59 = (s32[]{:T(128)}, bf16[3,864,4,64]{1,3,2,0:T(8,128)(2,1)}, bf16[3,864,4,64]{1,3,2,0:T(8,128)(2,1)}, bf16[3,864,4,64]{1,3,2,0:T(8,128)(2,1)}, bf16[3,8...) while((s32[]{:T(128)}, ...), condition=%wide.region_23.24_spmd.clone, body=%wide.region_21.23_spmd.clone.sunk | while | flops 1956259328 | bytes 134136328 | solution.py:135
  701.4 9.5 multiply_reduce_fusion.16
  710.9 6.9 multiply_convert_fusion.19
  728.2 9.5 multiply_reduce_fusion.16
  737.7 6.9 multiply_convert_fusion.19
  755.0 9.5 multiply_reduce_fusion.16
  764.5 6.9 multiply_convert_fusion.19
  775.9 8.7 convolution_convert_fusion.3
  785.9 11.3 convolution_convert_fusion.1
  799.0 9.6 convolution_convert_fusion.2
  810.4 8.4 fusion.134
  818.9 6.3 multiply_convert_fusion.2
  830.8 68.7 %reduce-scatter.57.cloned.1.call-done = bf16[96,1536]{1,0:T(8,128)(2,1)} async-done(((bf16[768,1536]{1,0:T(8,128)(2,1)}), bf16[96,1536]{1,0:T(8,128)(2,1)}) %reduce-scatter.57.cloned.1.call-update) | async-done | bytes 294928
  901.4 79.7 %reduce-scatter.33.cloned.1.call-done = bf16[96,2304]{1,0:T(8,128)(2,1)} async-done(((bf16[768,2304]{1,0:T(8,128)(2,1)}), bf16[96,2304]{1,0:T(8,128)(2,1)}) %reduce-scatter.33.cloned.1.call-update) | async-done | bytes 442384 | tf_op jit(solution)/shard_map/reduce_scatter | solution.py:305
  983.2 96.3 %reduce-scatter.47.cloned.1.call-done = bf16[384,768]{1,0:T(8,128)(2,1)} async-done(((bf16[3072,768]{1,0:T(8,128)(2,1)}), bf16[384,768]{1,0:T(8,128)(2,1)}) %reduce-scatter.47.cloned.1.call-update) | async-done | bytes 589840 | tf_op jit(solution)/shard_map/reduce_scatter | solution.py:323
  1081.8 96.3 %reduce-scatter.43.cloned.1.call-done = bf16[96,3072]{1,0:T(8,128)(2,1)} async-done(((bf16[768,3072]{1,0:T(8,128)(2,1)}), bf16[96,3072]{1,0:T(8,128)(2,1)}) %reduce-scatter.43.cloned.1.call-update) | async-done | bytes 589840 | tf_op jit(solution)/shard_map/reduce_scatter | solution.py:320
  1178.2 183.1 %reduce-scatter.31.cloned.1.call-done = bf16[96,6912]{1,0:T(8,128)(2,1)} async-done(((bf16[768,6912]{1,0:T(8,128)(2,1)}), bf16[96,6912]{1,0:T(8,128)(2,1)}) %reduce-scatter.31.cloned.1.call-update) | async-done | bytes 1327120 | tf_op jit(solution)/shard_map/reduce_scatter | solution.py:302
  1370.9 12.2 reduce-scatter.59.cloned.1.call-done
  1384.7 21.4 %reduce-scatter.55.cloned.1.call-done = bf16[192,96]{1,0:T(8,128)(2,1)} async-done(((bf16[768,96]{1,0:T(8,128)(2,1)}), bf16[192,96]{1,0:T(8,128)(2,1)}) %reduce-scatter.55.cloned.1.call-update) | async-done | bytes 36880
  1407.6 21.2 %reduce-scatter.53.cloned.1.call-done = bf16[192,96]{1,0:T(8,128)(2,1)} async-done(((bf16[768,96]{1,0:T(8,128)(2,1)}), bf16[192,96]{1,0:T(8,128)(2,1)}) %reduce-scatter.53.cloned.1.call-update) | async-done | bytes 36880
  1430.4 21.9 %reduce-scatter.39.cloned.1.call-done = bf16[96,384]{0,1:T(8,128)(2,1)} async-done(((bf16[96,1536]{0,1:T(8,128)(2,1)}), bf16[96,384]{0,1:T(8,128)(2,1)}) %reduce-scatter.39.cloned.1.call-update) | async-done | bytes 73744 | tf_op jit(solution)/shard_map/reduce_scatter | solution.py:340
  1454.0 23.7 %reduce-scatter.51.cloned.1.call-done = bf16[576,96]{1,0:T(8,128)(2,1)} async-done(((bf16[2304,96]{1,0:T(8,128)(2,1)}), bf16[576,96]{1,0:T(8,128)(2,1)}) %reduce-scatter.51.cloned.1.call-update) | async-done | bytes 110608
  1479.4 23.0 %reduce-scatter.61.cloned.1.call-done = bf16[192,384]{1,0:T(8,128)(2,1)} async-done(((bf16[768,384]{1,0:T(8,128)(2,1)}), bf16[192,384]{1,0:T(8,128)(2,1)}) %reduce-scatter.61.cloned.1.call-update) | async-done | bytes 147472
  1504.3 22.7 %reduce-scatter.45.cloned.1.call-done = bf16[96,768]{1,0:T(8,128)(2,1)} async-done(((bf16[96,3072]{1,0:T(8,128)(2,1)}), bf16[96,768]{1,0:T(8,128)(2,1)}) %reduce-scatter.45.cloned.1.call-update) | async-done | bytes 147472 | tf_op jit(solution)/shard_map/reduce_scatter | solution.py:346
  1528.7 30.5 %reduce-scatter.49.cloned.1.call-done = bf16[1728,96]{1,0:T(8,128)(2,1)} async-done(((bf16[6912,96]{1,0:T(8,128)(2,1)}), bf16[1728,96]{1,0:T(8,128)(2,1)}) %reduce-scatter.49.cloned.1.call-update) | async-done | bytes 331792
  (449 shorter events, 241.3 us)
Async XLA Ops:
  7.2 78.0 %copy-start = (bf16[1,256,768]{2,1,0:T(8,128)(2,1)S(1)}, bf16[1,256,768]{2,1,0:T(8,128)(2,1)}, u32[]{:S(2)}) copy-start(bf16[1,256,768]{2,1,0:T(8,128)(2,1)} %param.23) | copy-start | bytes 1179652
  7.2 23.7 %all-gather.28.cloned.1.call-start = ((), (), s32[]{:S(2)}) async-start(), calls=%async_computation.33 | async-start | bytes 1720320 | tf_op jit(solution)/shard_map/all_gather | solution.py:165
  7.9 77.2 %all-gather.18.cloned.1.call-start = ((), (), s32[]{:S(2)}) async-start(), calls=%async_computation.19 | async-start | bytes 2654208 | tf_op jit(solution)/shard_map/all_gather | solution.py:179
  17.0 222.0 %all-gather.12.cloned.1.call-start = ((), (), s32[]{:S(2)}) async-start(), calls=%async_computation.16 | async-start | bytes 11943936 | tf_op jit(solution)/shard_map/all_gather | solution.py:175
  35.3 269.7 %all-gather.14.cloned.1.call-start = ((), (), s32[]{:S(2)}) async-start(), calls=%async_computation.17 | async-start | bytes 3981312 | tf_op jit(solution)/shard_map/all_gather | solution.py:176
  35.3 28.6 %copy-start.40 = (bf16[96,768]{1,0:T(8,128)(2,1)S(1)}, bf16[96,768]{1,0:T(8,128)(2,1)}, u32[]{:S(2)}) copy-start(bf16[96,768]{1,0:T(8,128)(2,1)} %param.34) | copy-start | bytes 442372
  42.8 29.4 %copy-start.41 = (bf16[384,192]{0,1:T(8,128)(2,1)S(1)}, bf16[384,192]{0,1:T(8,128)(2,1)}, u32[]{:S(2)}) copy-start(bf16[384,192]{0,1:T(8,128)(2,1)} %param.35) | copy-start | bytes 442372
  44.0 37.7 %copy-start.6 = (bf16[1,864,768]{2,1,0:T(8,128)(2,1)S(1)}, bf16[1,864,768]{2,1,0:T(8,128)(2,1)}, u32[]{:S(2)}) copy-start(bf16[1,864,768]{2,1,0:T(8,128)(2,1)} %param.22) | copy-start | bytes 3981316
  44.0 315.0 %all-gather.16.cloned.1.call-start = ((), (), s32[]{:S(2)}) async-start(), calls=%async_computation.18 | async-start | bytes 1327104 | tf_op jit(solution)/shard_map/all_gather | solution.py:177
  50.7 338.9 %all-gather.20.cloned.1.call-start = ((), (), s32[]{:S(2)}) async-start(), calls=%async_computation.20 | async-start | bytes 1327104 | tf_op jit(solution)/shard_map/all_gather | solution.py:178
  57.3 374.9 %all-gather.22.cloned.1.call-start = ((), (), s32[]{:S(2)}) async-start(), calls=%async_computation.21 | async-start | bytes 1327104 | tf_op jit(solution)/shard_map/all_gather | solution.py:180
  63.9 449.2 %all-gather.24.cloned.1.call-start = ((), (), s32[]{:S(2)}) async-start(), calls=%async_computation.22 | async-start | bytes 5308416 | tf_op jit(solution)/shard_map/all_gather | solution.py:181
  72.1 522.3 %all-gather.26.cloned.1.call-start = ((), (), s32[]{:S(2)}) async-start(), calls=%async_computation.23 | async-start | bytes 5308416 | tf_op jit(solution)/shard_map/all_gather | solution.py:182
  80.3 745.0 %reduce-scatter.41.cloned.1.call-start = ((), (), s32[]{:S(2)}) async-start(), calls=%async_computation.29 | async-start | bytes 1327104 | tf_op jit(solution)/shard_map/reduce_scatter | solution.py:317
  81.9 223.0 %copy-start.48 = (f32[864]{0:T(1024)}, f32[864]{0:T(1024)S(1)}, u32[]{:S(2)}) copy-start(f32[864]{0:T(1024)S(1)} %broadcast_multiply_fusion.8) | copy-start | bytes 10372
  82.5 222.5 %copy-start.57 = (f32[864]{0:T(1024)}, f32[864]{0:T(1024)S(1)}, u32[]{:S(2)}) copy-start(f32[864]{0:T(1024)S(1)} %add_rsqrt_fusion.2) | copy-start | bytes 10372
  245.1 67.3 %copy-start.52 = (f32[768]{0:T(1024)}, f32[768]{0:T(1024)S(1)}, u32[]{:S(2)}) copy-start(f32[768]{0:T(1024)S(1)} %get-tuple-element.443) | copy-start | bytes 9220
  245.1 67.3 %copy-start.71 = (f32[768]{0:T(1024)}, f32[768]{0:T(1024)S(1)}, u32[]{:S(2)}) copy-start(f32[768]{0:T(1024)S(1)} %get-tuple-element.442) | copy-start | bytes 9220
  245.1 115.3 %copy-start.46 = (f32[768]{0:T(1024)}, f32[768]{0:T(1024)S(1)}, u32[]{:S(2)}) copy-start(f32[768]{0:T(1024)S(1)} %get-tuple-element.444) | copy-start | bytes 9220
  245.1 144.5 %copy-start.54 = (f32[768]{0:T(1024)}, f32[768]{0:T(1024)S(1)}, u32[]{:S(2)}) copy-start(f32[768]{0:T(1024)S(1)} %get-tuple-element.440) | copy-start | bytes 9220
  245.1 144.5 %copy-start.73 = (f32[768]{0:T(1024)}, f32[768]{0:T(1024)S(1)}, u32[]{:S(2)}) copy-start(f32[768]{0:T(1024)S(1)} %get-tuple-element.439) | copy-start | bytes 9220
  397.2 35.0 %copy-start.56 = (f32[768]{0:T(1024)S(1)}, f32[768]{0:T(1024)}, u32[]{:S(2)}) copy-start(f32[768]{0:T(1024)} %get-tuple-element.441) | copy-start | bytes 9220
  436.8 76.3 %copy-start.65 = (f32[768]{0:T(1024)S(1)}, f32[768]{0:T(1024)}, u32[]{:S(2)}) copy-start(f32[768]{0:T(1024)} %get-tuple-element.437) | copy-start | bytes 9220
  436.8 76.3 %copy-start.67 = (f32[768]{0:T(1024)S(1)}, f32[768]{0:T(1024)}, u32[]{:S(2)}) copy-start(f32[768]{0:T(1024)} %get-tuple-element.438) | copy-start | bytes 9220
  436.8 177.9 %copy-start.60 = (f32[864]{0:T(1024)}, f32[864]{0:T(1024)S(1)}, u32[]{:S(2)}) copy-start(f32[864]{0:T(1024)S(1)} %broadcast_multiply_fusion.6) | copy-start | bytes 10372
  438.8 175.9 %copy-start.75 = (f32[864]{0:T(1024)}, f32[864]{0:T(1024)S(1)}, u32[]{:S(2)}) copy-start(f32[864]{0:T(1024)S(1)} %add_rsqrt_fusion) | copy-start | bytes 10372
  513.1 81.2 %copy-start.69 = (f32[768]{0:T(1024)S(1)}, f32[768]{0:T(1024)}, u32[]{:S(2)}) copy-start(f32[768]{0:T(1024)} %get-tuple-element.436) | copy-start | bytes 9220
  632.6 194.5 %reduce-scatter.37.cloned.1.call-start = ((), (), s32[]{:S(2)}) async-start(), calls=%async_computation.27 | async-start | bytes 1327104 | tf_op jit(solution)/shard_map/reduce_scatter | solution.py:311
  672.7 156.2 %reduce-scatter.35.cloned.1.call-start = ((), (), s32[]{:S(2)}) async-start(), calls=%async_computation.26 | async-start | bytes 1327104 | tf_op jit(solution)/shard_map/reduce_scatter | solution.py:308
  683.2 216.2 %reduce-scatter.57.cloned.1.call-start = ((), (), s32[]{:S(2)}) async-start(), calls=%async_computation.38 | async-start | bytes 2654208
  691.2 289.9 %reduce-scatter.33.cloned.1.call-start = ((), (), s32[]{:S(2)}) async-start(), calls=%async_computation.25 | async-start | bytes 3981312 | tf_op jit(solution)/shard_map/reduce_scatter | solution.py:305
  695.3 80.6 %copy-start.49 = (f32[864]{0:T(1024)S(1)}, f32[864]{0:T(1024)}, u32[]{:S(2)}) copy-start(f32[864]{0:T(1024)} %copy-done.48) | copy-start | bytes 10372
  695.3 80.6 %copy-start.53 = (f32[768]{0:T(1024)S(1)}, f32[768]{0:T(1024)}, u32[]{:S(2)}) copy-start(f32[768]{0:T(1024)} %copy-done.52) | copy-start | bytes 9220
  695.3 80.6 %copy-start.58 = (f32[864]{0:T(1024)S(1)}, f32[864]{0:T(1024)}, u32[]{:S(2)}) copy-start(f32[864]{0:T(1024)} %copy-done.57) | copy-start | bytes 10372
  695.3 80.6 %copy-start.72 = (f32[768]{0:T(1024)S(1)}, f32[768]{0:T(1024)}, u32[]{:S(2)}) copy-start(f32[768]{0:T(1024)} %copy-done.71) | copy-start | bytes 9220
  784.6 295.0 %reduce-scatter.47.cloned.1.call-start = ((), (), s32[]{:S(2)}) async-start(), calls=%async_computation.32 | async-start | bytes 5308416 | tf_op jit(solution)/shard_map/reduce_scatter | solution.py:323
  797.3 380.8 %reduce-scatter.43.cloned.1.call-start = ((), (), s32[]{:S(2)}) async-start(), calls=%async_computation.30 | async-start | bytes 5308416 | tf_op jit(solution)/shard_map/reduce_scatter | solution.py:320
  808.7 552.5 %reduce-scatter.31.cloned.1.call-start = ((), (), s32[]{:S(2)}) async-start(), calls=%async_computation.24 | async-start | bytes 11943936 | tf_op jit(solution)/shard_map/reduce_scatter | solution.py:302
  825.2 557.9 %reduce-scatter.59.cloned.1.call-start = ((), (), s32[]{:S(2)}) async-start(), calls=%async_computation.39 | async-start | bytes 245760
  827.1 579.0 %reduce-scatter.55.cloned.1.call-start = ((), (), s32[]{:S(2)}) async-start(), calls=%async_computation.37 | async-start | bytes 245760
  828.9 599.9 %reduce-scatter.53.cloned.1.call-start = ((), (), s32[]{:S(2)}) async-start(), calls=%async_computation.36 | async-start | bytes 245760
  830.7 621.6 %reduce-scatter.39.cloned.1.call-start = ((), (), s32[]{:S(2)}) async-start(), calls=%async_computation.28 | async-start | bytes 491520 | tf_op jit(solution)/shard_map/reduce_scatter | solution.py:340
  901.3 576.3 %reduce-scatter.51.cloned.1.call-start = ((), (), s32[]{:S(2)}) async-start(), calls=%async_computation.35 | async-start | bytes 737280
  983.2 519.3 %reduce-scatter.61.cloned.1.call-start = ((), (), s32[]{:S(2)}) async-start(), calls=%async_computation.40 | async-start | bytes 737280
  1081.7 445.4 %reduce-scatter.45.cloned.1.call-start = ((), (), s32[]{:S(2)}) async-start(), calls=%async_computation.31 | async-start | bytes 737280 | tf_op jit(solution)/shard_map/reduce_scatter | solution.py:346
  1178.1 185.8 %copy-start.34 = (bf16[3,256,4,64]{1,3,2,0:T(8,128)(2,1)S(1)}, bf16[3,256,4,64]{1,3,2,0:T(8,128)(2,1)}, u32[]{:S(2)}) copy-start(bf16[3,256,4,64]{1,3,2,0:T(8,128)(2,1)} %get-tuple-element.204) | copy-start | bytes 1179652
  1178.1 185.8 %copy-start.38 = (bf16[3,256,4,64]{1,3,2,0:T(8,128)(2,1)S(1)}, bf16[3,256,4,64]{1,3,2,0:T(8,128)(2,1)}, u32[]{:S(2)}) copy-start(bf16[3,256,4,64]{1,3,2,0:T(8,128)(2,1)} %get-tuple-element.203) | copy-start | bytes 1179652
  1178.1 381.1 %reduce-scatter.49.cloned.1.call-start = ((), (), s32[]{:S(2)}) async-start(), calls=%async_computation.34 | async-start | bytes 2211840
  (91 other events, 444.8 us)
Sparse Core Ops, SparseCore 0:
  9.6 21.2 all-gather.27
  33.1 52.0 all-gather.17
  87.9 150.9 all-gather.11
  241.6 63.3 all-gather.13
  307.6 39.5 all-gather.15
  349.8 39.8 all-gather.19
  392.4 39.8 all-gather.21
  434.4 78.6 all-gather.23
  515.2 79.1 all-gather.25
  632.7 62.2 reduce-scatter.40
  698.4 63.0 reduce-scatter.36
  764.7 63.1 reduce-scatter.34
  831.4 67.9 reduce-scatter.56
  902.9 78.1 reduce-scatter.32
  984.6 94.9 reduce-scatter.46
  1083.1 94.9 reduce-scatter.42
  1181.5 179.6 reduce-scatter.30
  1364.3 18.8 reduce-scatter.58
  1386.3 19.7 reduce-scatter.54
  1409.1 19.7 reduce-scatter.52
  1431.5 20.7 reduce-scatter.38
  1455.5 22.0 reduce-scatter.50
  1480.3 22.0 reduce-scatter.60
  1504.9 22.0 reduce-scatter.44
  1529.8 29.3 reduce-scatter.48
where the time goes:
time: 1580 us; the launch traced here: 1570 us
  waiting for transfers between devices  1110 us (70%)
  matrix products  245 us (16%)
  local copies, waits for them, and re-layouts  79.8 us (5%)
  other arithmetic  63.6 us (4%)
  blocking collectives  49.3 us (3%)
  between operations  16 us (1%)
    unnamed x32, waiting for transfers between devices  202 us
    reduce_scatter x1, waiting for transfers between devices, body(): lax.psum_scatter(grad_ada.astype(jnp.bfloat16), 'dp', scatter_dimension=0...  183 us
    all_gather x1, waiting for transfers between devices, body(): lax.all_gather(columns[0], 'dp', axis=0, tiled=True)  150 us
    reduce_scatter x1, waiting for transfers between devices, body(): lax.psum_scatter(grad_fc1.astype(jnp.bfloat16), 'dp', scatter_dimension=0...  96.3 us
    reduce_scatter x1, waiting for transfers between devices, body(): lax.psum_scatter(grad_fc2.astype(jnp.bfloat16), 'dp', scatter_dimension=0...  96.3 us
    reduce_scatter x1, waiting for transfers between devices, body(): lax.psum_scatter(grad_qkv.astype(jnp.bfloat16), 'dp', scatter_dimension=0...  79.7 us
    all_gather x1, waiting for transfers between devices, body(): lax.all_gather(columns[6], 'dp', axis=0, tiled=True)  74.3 us
    all_gather x1, waiting for transfers between devices, body(): lax.all_gather(columns[7], 'dp', axis=0, tiled=True)  69.7 us
  transfers between devices with their start and end apart: 25, of which 21 were waited for; matrix products, arithmetic and copies ran while one was open for 21% of the time, Pallas kernels for 0%

commit v1 on v0

--- a/solution.py
+++ b/solution.py
@@ -1,8 +1,11 @@
+import functools
 import math
 
 import jax
 import jax.numpy as jnp
 from jax import lax
+from jax.experimental import pallas as pl
+from jax.experimental.pallas import tpu as pltpu
 from jax.sharding import PartitionSpec as P
 
 HEADS = 12
@@ -143,6 +146,379 @@
         ),
     )
     return (join_groups(query_grad), join_groups(key_grad), join_groups(value_grad))
+
+
+MESH = pl.DeviceIdType.MESH
+
+
+class Grid:
+    def __init__(self, dp_size, fsdp_size):
+        self.dp = dp_size
+        self.fsdp = fsdp_size
+        self.ny = 2
+        self.nz = dp_size // 2
+
+    def fits(self, matrices):
+        if self.fsdp != 4 or self.dp % 2:
+            return False
+        for matrix in matrices:
+            rows, columns = matrix.shape
+            if rows % 32 or (2 * columns) % 128:
+                return False
+        return True
+
+
+def pair_halves(matrix, core):
+    half = matrix.shape[0] // 2
+    mine = lax.dynamic_slice_in_dim(matrix, core * half, half, 0)
+    other = lax.dynamic_slice_in_dim(matrix, (1 - core) * half, half, 0)
+    return mine, other
+
+
+def core_swap(value, fsdp_size):
+    pairs = [(i, i ^ 1) for i in range(fsdp_size)]
+    return lax.ppermute(value, "fsdp", pairs)
+
+
+def place(nz):
+    dp_index = lax.axis_index("dp")
+    fsdp_index = lax.axis_index("fsdp")
+    return dp_index // 2, dp_index % 2, fsdp_index // 2, fsdp_index % 2
+
+
+def device(z, y, x, core):
+    return {"dp": z * 2 + y, "fsdp": x * 2 + core}
+
+
+def greet(partners):
+    barrier = pltpu.get_barrier_semaphore()
+    for partner in partners:
+        pl.semaphore_signal(barrier, inc=1, device_id=partner, device_id_type=MESH)
+    pl.semaphore_wait(barrier, len(partners))
+
+
+def gather_kernel(nz, count, *refs):
+    blocks = refs[:count]
+    wholes = refs[count : 2 * count]
+    local_sem, send_sem, recv_sem = refs[2 * count :]
+    z, y, x, core = place(nz)
+    sibling = device(z, y, x, 1 - core)
+    first = device(z, y * (1 - core) + (1 - y) * core, (1 - x) * (1 - core) + x * core, core)
+    second = device(z, (1 - y) * (1 - core) + y * core, x * (1 - core) + (1 - x) * core, core)
+    others = [device((z + step) % nz, y, x, core) for step in range(1, nz)]
+    greet([sibling, first, second, *others])
+
+    def columns(ref, which):
+        half = ref.shape[-1] // 2
+        return pl.ds(pl.multiple_of(which * half, 128), half)
+
+    def remote(item, slot, src, dst, partner):
+        return pltpu.make_async_remote_copy(
+            src_ref=src,
+            dst_ref=dst,
+            send_sem=send_sem.at[item, slot],
+            recv_sem=recv_sem.at[item, slot],
+            device_id=partner,
+            device_id_type=MESH,
+        )
+
+    def local(item):
+        whole = wholes[item]
+        return pltpu.make_async_copy(
+            blocks[item], whole.at[z, y, core, :, columns(whole, x)], local_sem.at[item]
+        )
+
+    def along_z(item):
+        whole = wholes[item]
+        spot = whole.at[z, y, core, :, columns(whole, x)]
+        return [
+            remote(item, step, blocks[item], spot, partner) for step, partner in enumerate(others)
+        ]
+
+    def stage_first(item):
+        whole = wholes[item]
+        part = whole.at[:, y, core, :, columns(whole, x)]
+        return [remote(item, nz - 1, part, part, first)]
+
+    def stage_second(item):
+        whole = wholes[item]
+        copies = []
+        for k in range(2):
+            row = y * (1 - core) + k * core
+            column = k * (1 - core) + x * core
+            part = whole.at[:, row, core, :, columns(whole, column)]
+            copies.append(remote(item, nz + k, part, part, second))
+        return copies
+
+    def stage_core(item):
+        part = wholes[item].at[:, :, core]
+        return [remote(item, nz + 2, part, part, sibling)]
+
+    stages = [along_z, stage_first, stage_second, stage_core]
+    for item in range(count):
+        local(item).start()
+        for copy in along_z(item):
+            copy.start()
+    for step in range(count + 3):
+        for depth in range(1, 4):
+            item = step - depth + 1
+            if 0 <= item < count:
+                if depth == 1:
+                    local(item).wait()
+                for copy in stages[depth - 1](item):
+                    copy.wait_recv()
+                for copy in stages[depth](item):
+                    copy.start()
+    for item in range(count):
+        for copy in stage_core(item):
+            copy.wait_recv()
+    for item in range(count):
+        for stage in stages:
+            for copy in stage(item):
+                copy.wait_send()
+
+
+def gather_weights(grid, matrices):
+    if not grid.fits(matrices):
+        return tuple(
+            lax.all_gather(lax.all_gather(m, "fsdp", axis=1, tiled=True), "dp", axis=0, tiled=True)
+            for m in matrices
+        )
+    core = lax.axis_index("fsdp") % 2
+    halves = [pair_halves(matrix, core) for matrix in matrices]
+    swapped = [core_swap(other, grid.fsdp) for _, other in halves]
+    blocks = []
+    for (mine, _), theirs in zip(halves, swapped):
+        both = jnp.where(
+            core == 0,
+            jnp.concatenate([mine, theirs], 1),
+            jnp.concatenate([theirs, mine], 1),
+        )
+        blocks.append(both)
+    count = len(blocks)
+    nz = grid.nz
+    shapes = [
+        jax.ShapeDtypeStruct((nz, 2, 2, b.shape[0], b.shape[1] * 2), b.dtype) for b in blocks
+    ]
+    wholes = pl.pallas_call(
+        functools.partial(gather_kernel, nz, count),
+        out_shape=shapes,
+        in_specs=[pl.BlockSpec(memory_space=pl.ANY)] * count,
+        out_specs=[pl.BlockSpec(memory_space=pl.ANY)] * count,
+        scratch_shapes=[
+            pltpu.SemaphoreType.DMA((count,)),
+            pltpu.SemaphoreType.DMA((count, nz + 3)),
+            pltpu.SemaphoreType.DMA((count, nz + 3)),
+        ],
+        compiler_params=pltpu.CompilerParams(collective_id=0, has_side_effects=True),
+        name="gather_weights",
+    )(*blocks)
+    return tuple(w.reshape(-1, w.shape[-1]) for w in wholes)
+
+
+def reduce_kernel(nz, count, *refs):
+    grads = refs[:count]
+    sums = refs[count : 2 * count]
+    rest = refs[2 * count :]
+    kept, from_core, from_first, from_second, from_z = (
+        rest[i * count : (i + 1) * count] for i in range(5)
+    )
+    local_sem, send_sem, recv_sem = rest[5 * count :]
+    z, y, x, core = place(nz)
+    sibling = device(z, y, x, 1 - core)
+    first = device(z, (1 - y) * (1 - core) + y * core, x * (1 - core) + (1 - x) * core, core)
+    second = device(z, y * (1 - core) + (1 - y) * core, (1 - x) * (1 - core) + x * core, core)
+    others = [((z + step) % nz, step) for step in range(1, nz)]
+    greet([sibling, first, second, *[device(other, y, x, core) for other, _ in others]])
+
+    def columns(ref, which):
+        half = ref.shape[-1] // 2
+        return pl.ds(pl.multiple_of(which * half, 128), half)
+
+    def remote(item, slot, src, dst, partner):
+        return pltpu.make_async_remote_copy(
+            src_ref=src,
+            dst_ref=dst,
+            send_sem=send_sem.at[item, slot],
+            recv_sem=recv_sem.at[item, slot],
+            device_id=partner,
+            device_id_type=MESH,
+        )
+
+    def local(item):
+        return pltpu.make_async_copy(grads[item].at[:, :, core], kept[item], local_sem.at[item])
+
+    def stage_core(item):
+        return [remote(item, nz + 2, grads[item].at[:, :, 1 - core], from_core[item], sibling)]
+
+    def stage_first(item):
+        copies = []
+        for k in range(2):
+            row = (1 - y) * (1 - core) + k * core
+            column = k * (1 - core) + (1 - x) * core
+            part = kept[item].at[:, row, :, columns(kept[item], column)]
+            copies.append(remote(item, nz + k, part, from_first[item].at[:, k], first))
+        return copies
+
+    def stage_second(item):
+        row = y * (1 - core) + (1 - y) * core
+        column = (1 - x) * (1 - core) + x * core
+        part = kept[item].at[:, row, :, columns(kept[item], column)]
+        return [remote(item, nz - 1, part, from_second[item], second)]
+
+    def along_z(item):
+        copies = []
+        for other, step in others:
+            part = kept[item].at[other, y, :, columns(kept[item], x)]
+            copies.append(
+                remote(item, step - 1, part, from_z[item].at[step - 1], device(other, y, x, core))
+            )
+        return copies
+
+    def add_core(item):
+        def one(step, carry):
+            a, b = step // 2, step % 2
+            kept[item][a, b] = (
+                kept[item][a, b].astype(jnp.float32) + from_core[item][a, b].astype(jnp.float32)
+            ).astype(jnp.bfloat16)
+            return carry
+
+        lax.fori_loop(0, nz * 2, one, 0)
+
+    def add_first(item):
+        for k in range(2):
+            row = y * (1 - core) + k * core
+            column = columns(kept[item], k * (1 - core) + x * core)
+
+            def one(a, carry):
+                kept[item][a, row, :, column] = (
+                    kept[item][a, row, :, column].astype(jnp.float32)
+                    + from_first[item][a, k].astype(jnp.float32)
+                ).astype(jnp.bfloat16)
+                return carry
+
+            lax.fori_loop(0, nz, one, 0)
+
+    def add_second(item):
+        column = columns(kept[item], x)
+
+        def one(a, carry):
+            kept[item][a, y, :, column] = (
+                kept[item][a, y, :, column].astype(jnp.float32)
+                + from_second[item][a].astype(jnp.float32)
+            ).astype(jnp.bfloat16)
+            return carry
+
+        lax.fori_loop(0, nz, one, 0)
+
+    def add_z(item):
+        total = kept[item][z, y, :, columns(kept[item], x)].astype(jnp.float32)
+        for step in range(nz - 1):
+            total += from_z[item][step].astype(jnp.float32)
+        sums[item][...] = total
+
+    stages = [stage_core, stage_first, stage_second, along_z]
+    adds = [add_core, add_first, add_second, add_z]
+    for item in range(count):
+        local(item).start()
+        for copy in stage_core(item):
+            copy.start()
+    for step in range(count + 3):
+        for depth in range(4):
+            item = step - depth
+            if 0 <= item < count:
+                if depth == 0:
+                    local(item).wait()
+                for copy in stages[depth](item):
+                    copy.wait_recv()
+                adds[depth](item)
+                if depth < 3:
+                    for copy in stages[depth + 1](item):
+                        copy.start()
+    for item in range(count):
+        for stage in stages:
+            for copy in stage(item):
+                copy.wait_send()
+
+
+def reduce_gradients(grid, gradients):
+    rounded = [g.astype(jnp.bfloat16) for g in gradients]
+    blocks = [
+        jax.ShapeDtypeStruct((g.shape[0] // grid.dp, g.shape[1] // grid.fsdp), jnp.bfloat16)
+        for g in gradients
+    ]
+    if not grid.fits(blocks):
+        out = []
+        for g in rounded:
+            part = lax.psum_scatter(g, "dp", scatter_dimension=0, tiled=True)
+            part = lax.psum_scatter(part, "fsdp", scatter_dimension=1, tiled=True)
+            out.append(part.astype(jnp.float32))
+        return tuple(out)
+    nz = grid.nz
+    count = len(rounded)
+    shaped = [g.reshape(nz, 2, 2, g.shape[0] // (nz * 4), g.shape[1]) for g in rounded]
+    rows = [g.shape[3] for g in shaped]
+    widths = [g.shape[4] for g in shaped]
+    bf16 = jnp.bfloat16
+    scratch = [pltpu.VMEM((nz, 2, r, w), bf16) for r, w in zip(rows, widths)]
+    scratch += [pltpu.VMEM((nz, 2, r, w), bf16) for r, w in zip(rows, widths)]
+    scratch += [pltpu.VMEM((nz, 2, r, w // 2), bf16) for r, w in zip(rows, widths)]
+    scratch += [pltpu.VMEM((nz, r, w // 2), bf16) for r, w in zip(rows, widths)]
+    scratch += [pltpu.VMEM((nz - 1, r, w // 2), bf16) for r, w in zip(rows, widths)]
+    scratch += [
+        pltpu.SemaphoreType.DMA((count,)),
+        pltpu.SemaphoreType.DMA((count, nz + 3)),
+        pltpu.SemaphoreType.DMA((count, nz + 3)),
+    ]
+    sums = pl.pallas_call(
+        functools.partial(reduce_kernel, nz, count),
+        out_shape=[
+            jax.ShapeDtypeStruct((r, w // 2), jnp.float32) for r, w in zip(rows, widths)
+        ],
+        in_specs=[pl.BlockSpec(memory_space=pl.ANY)] * count,
+        out_specs=[pl.BlockSpec(memory_space=pltpu.VMEM)] * count,
+        scratch_shapes=scratch,
+        compiler_params=pltpu.CompilerParams(
+            collective_id=1, has_side_effects=True, vmem_limit_bytes=56 * 1024 * 1024
+        ),
+        name="reduce_gradients",
+    )(*shaped)
+    core = lax.axis_index("fsdp") % 2
+    out = []
+    for total in sums:
+        half = total.shape[1] // 2
+        mine = lax.dynamic_slice_in_dim(total, core * half, half, 1)
+        other = lax.dynamic_slice_in_dim(total, (1 - core) * half, half, 1)
+        theirs = core_swap(other, grid.fsdp)
+        out.append(
+            jnp.where(
+                core == 0,
+                jnp.concatenate([mine, theirs], 0),
+                jnp.concatenate([theirs, mine], 0),
+            )
+        )
+    return tuple(out)
+
+
+def modulate(grid, timestep, w_ada):
+    rows, columns = w_ada.shape
+    model_width = rows * grid.dp
+    times = lax.all_gather(timestep, ("dp", "fsdp"), axis=0, tiled=True)
+    conditions = jax.nn.silu(
+        jax.vmap(lambda value: sinusoid(value, model_width))(times)
+    ).astype(jnp.bfloat16)
+    mine = lax.dynamic_slice_in_dim(conditions, lax.axis_index("dp") * rows, rows, 1)
+    partial = jnp.dot(mine, w_ada, preferred_element_type=jnp.float32)
+    summed = lax.psum_scatter(partial, "dp", scatter_dimension=0, tiled=True)
+    mixed = lax.all_to_all(summed, "fsdp", split_axis=0, concat_axis=0, tiled=True)
+    return mine, mixed.reshape(9, model_width)
+
+
+def ada_gradient(grid, conditions, dmodulation):
+    spread = dmodulation.reshape(grid.fsdp, -1)
+    swapped = lax.all_to_all(spread, "fsdp", split_axis=0, concat_axis=0, tiled=True)
+    everyone = lax.all_gather(swapped, "dp", axis=0, tiled=True)
+    return outer_sum(conditions, everyone)
 
 
 def body(
@@ -160,28 +536,16 @@
     w_cout,
     w_fc1,
     w_fc2,
+    *,
+    dp_size,
+    fsdp_size,
 ):
-    columns = (
-        lax.all_gather(w_ada, "fsdp", axis=1, tiled=True),
-        lax.all_gather(w_qkv, "fsdp", axis=1, tiled=True),
-        lax.all_gather(w_out, "fsdp", axis=1, tiled=True),
-        lax.all_gather(w_cq, "fsdp", axis=1, tiled=True),
-        lax.all_gather(w_ckv, "fsdp", axis=1, tiled=True),
-        lax.all_gather(w_cout, "fsdp", axis=1, tiled=True),
-        lax.all_gather(w_fc1, "fsdp", axis=1, tiled=True),
-        lax.all_gather(w_fc2, "fsdp", axis=1, tiled=True),
-    )
-    weights = (
-        lax.all_gather(columns[0], "dp", axis=0, tiled=True),
-        lax.all_gather(columns[1], "dp", axis=0, tiled=True),
-        lax.all_gather(columns[2], "dp", axis=0, tiled=True),
-        lax.all_gather(columns[3], "dp", axis=0, tiled=True),
-        lax.all_gather(columns[4], "dp", axis=0, tiled=True),
-        lax.all_gather(columns[5], "dp", axis=0, tiled=True),
-        lax.all_gather(columns[6], "dp", axis=0, tiled=True),
-        lax.all_gather(columns[7], "dp", axis=0, tiled=True),
-    )
-    full_ada, full_qkv, full_out, full_cq, full_ckv, full_cout, full_fc1, full_fc2 = weights
+    grid = Grid(dp_size, fsdp_size)
+    matrices = (w_qkv, w_out, w_cq, w_ckv, w_cout, w_fc1, w_fc2)
+    full_qkv, full_out, full_cq, full_ckv, full_cout, full_fc1, full_fc2 = gather_weights(
+        grid, matrices
+    )
+    conditions, modulation = modulate(grid, timestep, w_ada)
     latent = latents[0].astype(jnp.float32)
     text_block = text_rows[0]
     slot_count = latent.shape[0]
@@ -190,10 +554,6 @@
     head_size = model_width // HEADS
     frame_valid = jnp.arange(slot_count) < frame_len[0]
     text_valid = jnp.arange(text_slots) < text_len[0]
-    condition = jax.nn.silu(sinusoid(timestep[0], model_width)).astype(jnp.bfloat16)
-    modulation = jnp.dot(condition[None, :], full_ada, preferred_element_type=jnp.float32).reshape(
-        9, model_width
-    )
     normed_one, inverse_one = normalize(latent)
     hidden_one = (normed_one * (1.0 + modulation[1]) + modulation[0]).astype(jnp.bfloat16)
     packed = jnp.dot(hidden_one, full_qkv, preferred_element_type=jnp.float32).astype(jnp.bfloat16)
@@ -218,27 +578,6 @@
     activated = gelu_tanh(pre_gelu).astype(jnp.bfloat16)
     branch_three = jnp.dot(activated, full_fc2, preferred_element_type=jnp.float32)
     layer_out = after_cross + modulation[8] * branch_three
-    columns = (
-        lax.all_gather(w_ada, "fsdp", axis=1, tiled=True),
-        lax.all_gather(w_qkv, "fsdp", axis=1, tiled=True),
-        lax.all_gather(w_out, "fsdp", axis=1, tiled=True),
-        lax.all_gather(w_cq, "fsdp", axis=1, tiled=True),
-        lax.all_gather(w_ckv, "fsdp", axis=1, tiled=True),
-        lax.all_gather(w_cout, "fsdp", axis=1, tiled=True),
-        lax.all_gather(w_fc1, "fsdp", axis=1, tiled=True),
-        lax.all_gather(w_fc2, "fsdp", axis=1, tiled=True),
-    )
-    weights = (
-        lax.all_gather(columns[0], "dp", axis=0, tiled=True),
-        lax.all_gather(columns[1], "dp", axis=0, tiled=True),
-        lax.all_gather(columns[2], "dp", axis=0, tiled=True),
-        lax.all_gather(columns[3], "dp", axis=0, tiled=True),
-        lax.all_gather(columns[4], "dp", axis=0, tiled=True),
-        lax.all_gather(columns[5], "dp", axis=0, tiled=True),
-        lax.all_gather(columns[6], "dp", axis=0, tiled=True),
-        lax.all_gather(columns[7], "dp", axis=0, tiled=True),
-    )
-    full_ada, full_qkv, full_out, full_cq, full_ckv, full_cout, full_fc1, full_fc2 = weights
     upstream = out_grad[0].astype(jnp.float32)
     dbranch_three = (modulation[8] * upstream).astype(jnp.bfloat16)
     dgate_three = jnp.sum(upstream * branch_three, 0)
@@ -297,59 +636,11 @@
         .reshape(1, -1)
         .astype(jnp.bfloat16)
     )
-    grad_ada = outer_sum(condition[None, :], dmodulation)
-    reduced = (
-        lax.psum_scatter(
-            grad_ada.astype(jnp.bfloat16), "dp", scatter_dimension=0, tiled=True
-        ).astype(jnp.float32),
-        lax.psum_scatter(
-            grad_qkv.astype(jnp.bfloat16), "dp", scatter_dimension=0, tiled=True
-        ).astype(jnp.float32),
-        lax.psum_scatter(
-            grad_out.astype(jnp.bfloat16), "dp", scatter_dimension=0, tiled=True
-        ).astype(jnp.float32),
-        lax.psum_scatter(
-            grad_cq.astype(jnp.bfloat16), "dp", scatter_dimension=0, tiled=True
-        ).astype(jnp.float32),
-        lax.psum_scatter(
-            grad_ckv.astype(jnp.bfloat16), "dp", scatter_dimension=0, tiled=True
-        ).astype(jnp.float32),
-        lax.psum_scatter(
-            grad_cout.astype(jnp.bfloat16), "dp", scatter_dimension=0, tiled=True
-        ).astype(jnp.float32),
-        lax.psum_scatter(
-            grad_fc1.astype(jnp.bfloat16), "dp", scatter_dimension=0, tiled=True
-        ).astype(jnp.float32),
-        lax.psum_scatter(
-            grad_fc2.astype(jnp.bfloat16), "dp", scatter_dimension=0, tiled=True
-        ).astype(jnp.float32),
-    )
-    owned_grads = (
-        lax.psum_scatter(
-            reduced[0].astype(jnp.bfloat16), "fsdp", scatter_dimension=1, tiled=True
-        ).astype(jnp.float32),
-        lax.psum_scatter(
-            reduced[1].astype(jnp.bfloat16), "fsdp", scatter_dimension=1, tiled=True
-        ).astype(jnp.float32),
-        lax.psum_scatter(
-            reduced[2].astype(jnp.bfloat16), "fsdp", scatter_dimension=1, tiled=True
-        ).astype(jnp.float32),
-        lax.psum_scatter(
-            reduced[3].astype(jnp.bfloat16), "fsdp", scatter_dimension=1, tiled=True
-        ).astype(jnp.float32),
-        lax.psum_scatter(
-            reduced[4].astype(jnp.bfloat16), "fsdp", scatter_dimension=1, tiled=True
-        ).astype(jnp.float32),
-        lax.psum_scatter(
-            reduced[5].astype(jnp.bfloat16), "fsdp", scatter_dimension=1, tiled=True
-        ).astype(jnp.float32),
-        lax.psum_scatter(
-            reduced[6].astype(jnp.bfloat16), "fsdp", scatter_dimension=1, tiled=True
-        ).astype(jnp.float32),
-        lax.psum_scatter(
-            reduced[7].astype(jnp.bfloat16), "fsdp", scatter_dimension=1, tiled=True
-        ).astype(jnp.float32),
-    )
+    grad_ada = ada_gradient(grid, conditions, dmodulation)
+    owned = reduce_gradients(
+        grid, (grad_qkv, grad_out, grad_cq, grad_ckv, grad_cout, grad_fc1, grad_fc2)
+    )
+    owned_grads = (grad_ada, *owned)
     return (
         layer_out[None],
         latent_grad[None],
@@ -383,7 +674,7 @@
         P("dp", "fsdp"),
     )
     return jax.shard_map(
-        body,
+        functools.partial(body, dp_size=mesh.shape["dp"], fsdp_size=mesh.shape["fsdp"]),
         mesh=mesh,
         in_specs=placed,
         out_specs=(

time: 1580 us -> 676 us (0.43)
  waiting for transfers between devices: 1110 us -> 3.14 us
  Pallas kernels: 0 us -> 217 us
  blocking collectives: 49.3 us -> 74.9 us
  local copies, waits for them, and re-layouts: 79.8 us -> 54.6 us
  matrix products: 245 us -> 227 us
    reduce_scatter x9 -> x0, waiting for transfers between devices: 500 us -> none  [the longest x1 183 us: body(): lax.psum_scatter(grad_ada.astype(jnp.bfloat16), 'dp', scatter_dimension=0...]
    all_gather x9 -> x0, waiting for transfers between devices: 409 us -> none  [the longest x1 150 us: body(): lax.all_gather(columns[0], 'dp', axis=0, tiled=True)]
    pallas_call x0 -> x2, Pallas kernels: none -> 217 us  [the longest x1 113 us: reduce_gradients(): pl.pallas_call(functools.partial(reduce_kernel, nz, count), out_shape=[ja...]
    unnamed x32 -> x2, waiting for transfers between devices: 202 us -> 0.04 us
    unnamed x0 -> x1, blocking collectives: none -> 41.5 us
    unnamed x165 -> x148, local copies, waits for them, and re-layouts: 38.6 us -> 5.94 us
    all_gather x7 -> x1, blocking collectives: 49.3 us -> 33.4 us  [ada_gradient(): everyone = lax.all_gather(swapped, 'dp', axis=0, tiled=True)]
    dot_general x7 -> x8, matrix products: 39.5 us -> 38.5 us  [outer_sum(): lax.dot_general(left, right, (((0,), (0,)), ((), ())), preferred_element_...]
  transfers between devices with their start and end apart: 25 -> 17, of which waited for: 21 -> 1; matrix products, arithmetic and copies ran while one was open for 21% -> 5% of each run, Pallas kernels for 0% -> 32%
where the time goes in v1:
time: 676 us; the launch traced here: 670 us
  matrix products  227 us (34%)
  Pallas kernels  217 us (32%)
  blocking collectives  74.9 us (11%)
  other arithmetic  63.4 us (9%)
  local copies, waits for them, and re-layouts  54.6 us (8%)
  between operations  16.6 us (2%)
  starting transfers between devices  11.2 us (2%)
    pallas_call x1, Pallas kernels, reduce_gradients(): pl.pallas_call(functools.partial(reduce_kernel, nz, count), out_shape=[ja...  113 us
    pallas_call x1, Pallas kernels, gather_weights(): pl.pallas_call(functools.partial(gather_kernel, nz, count), out_shape=sha...  104 us
    unnamed x1, blocking collectives  41.5 us
    dot_general x7, matrix products, through(): lax.dot_general(gradient, matrix, (((1,), (1,)), ((), ())), preferred_ele...  39.5 us
    dot_general x8, matrix products, outer_sum(): lax.dot_general(left, right, (((0,), (0,)), ((), ())), preferred_element_...  38.5 us
    dot_general x6, matrix products, one_group(): jnp.einsum('shd,thd->hst', upstream_part, value_part, preferred_element_t...  33.6 us
    all_gather x1, blocking collectives, ada_gradient(): everyone = lax.all_gather(swapped, 'dp', axis=0, tiled=True)  33.4 us
    dot_general x6, matrix products, one_group(): jnp.einsum('hst,thd->shd', shares, value_part, preferred_element_type=jnp...  24.2 us
  transfers between devices with their start and end apart: 17, of which 1 were waited for; matrix products, arithmetic and copies ran while one was open for 5% of the time, Pallas kernels for 32%

profile of v1, /device:TPU:0, one launch (start us, length us, event | category | flops | bytes accessed | tf_op | source)
XLA Modules:
  0.0 669.7 jit_solution(3194309058073502272)
XLA Ops:
  13.8 41.5 %all-reduce = s32[32]{0:T(128)S(1)} all-reduce(s32[32]{0:T(128)S(1)} %dynamic-update-slice), channel_id=1, replica_groups=mesh['dp'=8,'fsdp'=4] {'dp','fsdp'}, use_global_device_ids=true, to_apply=%add | all-reduce | flops 32 | bytes 256
  66.4 103.9 %gather_weights.1 = (bf16[4,2,2,48,2304]{4,3,2,1,0:T(8,128)(2,1)}, bf16[4,2,2,48,768]{4,3,2,1,0:T(8,128)(2,1)}, bf16[4,2,2,48,768]{4,3,2,1,0:T(8,128)(2,1)}, bf1...) custom-call(bf16[48,1152]{1,0:T(8,128)(2,1)} %maximum_select_fusion., ...), custom_call_target="tpu_custom_call" | custom-call | tf_op jit(solution)/shard_map/gather_weights/pallas_call | solution.py:303
  174.3 3.5 all-to-all-start
  178.6 3.1 all-to-all-done
  182.5 7.2 %convolution_convert_fusion = bf16[864,2304]{1,0:T(8,128)(2,1)} fusion(bf16[768,2304]{1,0:T(8,128)(2,1)} %bitcast.417, bf16[1,864,768]{2,1,0:T(8,128)(2,1)S(1)} %copy-done.6, f32[768]{0:T(1024)S(1)} %get-tuple-element.375, f32[768]{0:T(1024)S(1)} %get-tuple-element.376, f32[864]{0:T(1024)S(1)} %add_rsqrt_fusion.2, f32[864]{0:T(1024)S(1)} %broadcast_multiply_fusion.8), kind=kOutput, calls=%fused_computation.132 | convolution fusion | flops 3063619584 | bytes 8860416 | tf_op jit(solution)/shard_map/dot_general | solution.py:559
  189.7 6.4 copy.68
  196.1 3.7 fusion.185
  201.8 36.7 %while.56 = (s32[]{:T(128)}, bf16[3,864,4,64]{1,3,2,0:T(8,128)(2,1)}, f32[3,4,864]{2,1,0:T(4,128)}, bf16[3,864,4,64]{1,3,2,0:T(8,128)(2,1)}, bf16[3,864,4,64]{1,...) while((s32[]{:T(128)}, ...), condition=%wide.region_6.7_spmd.clone, body=%wide.region_3.6_spmd.clone.sunk | while | flops 800462336 | bytes 37783684 | solution.py:92
  202.4 2.6 fusion.247
  205.0 3.1 fusion.248
  208.1 5.2 fusion.249
  214.6 2.6 fusion.247
  217.2 3.1 fusion.248
  220.3 5.2 fusion.249
  226.7 2.6 fusion.247
  229.4 3.1 fusion.248
  232.4 5.2 fusion.249
  240.0 4.9 fusion.183
  252.5 20.1 %while.57 = (s32[]{:T(128)}, bf16[3,864,4,64]{1,3,2,0:T(8,128)(2,1)}, f32[3,4,864]{2,1,0:T(4,128)S(1)}, bf16[3,256,4,64]{1,3,2,0:T(8,128)(2,1)}, bf16[3,864,4,64...) while((s32[]{:T(128)}, ...), condition=%wide.region_12.13_spmd.clone, body=%wide.region_9.12_spmd.clone.sunk | while | flops 237327232 | bytes 11912037 | solution.py:92
  256.3 2.9 fusion.253
  263.0 2.9 fusion.253
  269.7 2.9 fusion.253
  272.6 3.3 fusion.182
  276.7 7.3 %fusion.179 = f32[864,3072]{1,0:T(8,128)} fusion(bf16[768,3072]{1,0:T(8,128)(2,1)S(1)} %bitcast.415, f32[864,768]{1,0:T(8,128)S(1)} %get-tuple-element.451, f32[768]{0:T(1024)S(1)} %copy-done.65, f32[768]{0:T(1024)S(1)} %copy-done.64, f32[864]{0:T(1024)S(1)} %add_rsqrt_fusion, f32[864]{0:T(1024)S(1)} %broadcast_multiply_fusion.6), kind=kOutput, calls=%fused_computation.297 | convolution fusion | flops 4080181248 | bytes 18002688 | tf_op jit(solution)/shard_map/dot_general | solution.py:577
  283.9 11.8 %convolution_convert_fusion.1 = bf16[3072,768]{1,0:T(8,128)(2,1)} fusion(bf16[1,864,768]{2,1,0:T(8,128)(2,1)S(1)} %copy-done.73, f32[768]{0:T(1024)S(1)} %copy-done.63, f32[864,3072]{1,0:T(8,128)} %fusion.179), kind=kOutput, calls=%fused_computation.133 | convolution fusion | flops 4105101312 | bytes 16665600 | tf_op jit(solution)/shard_map/dot_general | solution.py:44
  295.7 12.7 %fusion.117 = bf16[864,3072]{1,0:T(8,128)(2,1)} fusion(f32[864,3072]{1,0:T(8,128)} %fusion.179, bf16[3072,768]{1,0:T(8,128)(2,1)S(1)} %bitcast.411, bf16[1,864,768]{2,1,0:T(8,128)(2,1)S(1)} %copy-done.73, f32[768]{0:T(1024)S(1)} %copy-done.63), kind=kOutput, calls=%fused_computation.130 | convolution fusion | flops 4131938304 | bytes 21974016 | tf_op jit(solution)/shard_map/dot_general | solution.py:50
  308.4 9.5 %multiply_reduce_fusion.2 = (bf16[768]{0:T(1024)(128)(2,1)}, f32[864]{0:T(1024)S(1)}, f32[864]{0:T(1024)S(1)}, bf16[768]{0:T(1024)(128)(2,1)}, f32[864,768]{1,0:T(8,128)}) fusion(f32[864,768]{1,0:T(8,128)S(1)} %get-tuple-element.451, f32[864]{0:T(1024)S(1)} %add_rsqrt_fusion, f32[864]{0:T(1024)S(1)} %broadcast_multiply_fusion.6, f32[768]{0:T(1024)S(1)} %copy-done.64, ...), kind=kOutput, calls=%fused_computation.170 | convolution fusion | flops 4082832384 | bytes 15355392 | tf_op jit(solution)/shard_map/dot_general | solution.py:50
  317.9 7.9 %convolution_convert_fusion.2 = bf16[768,3072]{1,0:T(8,128)(2,1)} fusion(bf16[864,3072]{1,0:T(8,128)(2,1)S(1)} %copy-done.78, f32[864,768]{1,0:T(8,128)S(1)} %get-tuple-element.451, f32[768]{0:T(1024)S(1)} %copy-done.65, f32[768]{0:T(1024)S(1)} %copy-done.64, f32[864]{0:T(1024)S(1)} %add_rsqrt_fusion, f32[864]{0:T(1024)S(1)} %broadcast_multiply_fusion.6), kind=kOutput, calls=%fused_computation.134 | convolution fusion | flops 4082540544 | bytes 12694272 | tf_op jit(solution)/shard_map/dot_general | solution.py:44
  325.8 11.4 %fusion.138 = (bf16[768]{0:T(1024)(128)(2,1)}, f32[1,864,768]{2,1,0:T(8,128)}, bf16[768]{0:T(1024)(128)(2,1)}, f32[864,768]{1,0:T(8,128)S(1)}) fusion(bf16[1,864,768]{2,1,0:T(8,128)(2,1)S(1)} %copy-done.74, f32[864,768]{1,0:T(8,128)S(1)} %get-tuple-element.451, f32[768]{0:T(1024)S(1)} %copy-done.63, f32[864,768]{1,0:T(8,128)S(1)} %get-tuple-element.502, ...), kind=kOutput, calls=%fused_computation.163 | convolution fusion | flops 4110703104 | bytes 29956608 | tf_op jit(solution)/shard_map/dot_general | solution.py:579
  345.8 27.9 %while.58 = (s32[]{:T(128)}, bf16[3,864,4,64]{1,3,2,0:T(8,128)(2,1)}, bf16[3,256,4,64]{1,3,2,0:T(8,128)(2,1)}, bf16[3,256,4,64]{1,3,2,0:T(8,128)(2,1)}, bf16[3,2...) while((s32[]{:T(128)}, ...), condition=%wide.region_19.20_spmd.clone, body=%wide.region_17.19_spmd.clone.sunk | while | flops 574477184 | bytes 52504640 | solution.py:138
  373.7 4.3 convolution_convert_fusion.10
  378.0 2.8 multiply_reduce_fusion.4
  391.8 80.7 %while.59 = (s32[]{:T(128)}, bf16[3,864,4,64]{1,3,2,0:T(8,128)(2,1)}, bf16[3,864,4,64]{1,3,2,0:T(8,128)(2,1)}, bf16[3,864,4,64]{1,3,2,0:T(8,128)(2,1)}, bf16[3,8...) while((s32[]{:T(128)}, ...), condition=%wide.region_24.25_spmd.clone, body=%wide.region_22.24_spmd.clone.sunk | while | flops 1956259328 | bytes 134136328 | solution.py:138
  395.4 2.9 fusion.277
  398.4 9.5 %multiply_reduce_fusion.16 = (f32[4,864]{1,0:T(4,128)S(1)}, f32[4,864,864]{1,2,0:T(8,128)}) fusion(f32[4,864,864]{1,2,0:T(8,128)S(1)} %fusion.274, f32[4,864]{1,0:T(4,128)S(1)} %dynamic-slice_bitcast_fusion.6, pred[864]{0:T(1024)(128)(4,1)S(1)} %iota_compare_fusion.11, bf16[3,864,4,64]{1,3,2,0:T(8,128)(2,1)} %get-tuple-element.843, s32[]{:T(128)S(6)} %copy.131, ...), kind=kOutput, calls=%fused_computation.84.clone.1 | convolution fusion | flops 397132416 | bytes 25277952 | tf_op jit(solution)/shard_map/while/body/eval_jaxpr/shd,thd->hst/dot_general | solution.py:116
  407.8 6.9 %multiply_convert_fusion.19 = bf16[4,864,864]{1,2,0:T(8,128)(2,1)S(1)} fusion(f32[4,864,864]{1,2,0:T(8,128)} %get-tuple-element.730, f32[4,864,864]{1,2,0:T(8,128)S(1)} %fusion.274, f32[4,864]{1,0:T(4,128)S(1)} %get-tuple-element.731, f32[4,864]{1,0:T(4,128)S(1)} %dynamic-slice_bitcast_fusion.6, pred[864]{0:T(1024)(128)(4,1)S(1)} %iota_compare_fusion.11), kind=kLoop, calls=%fused_computation.83.clone.1 | loop fusion | flops 17915904 | bytes 29888352 | tf_op jit(solution)/shard_map/while/body/eval_jaxpr/convert_element_type | solution.py:121
  422.2 2.9 fusion.277
  425.1 9.5 %multiply_reduce_fusion.16 = (f32[4,864]{1,0:T(4,128)S(1)}, f32[4,864,864]{1,2,0:T(8,128)}) fusion(f32[4,864,864]{1,2,0:T(8,128)S(1)} %fusion.274, f32[4,864]{1,0:T(4,128)S(1)} %dynamic-slice_bitcast_fusion.6, pred[864]{0:T(1024)(128)(4,1)S(1)} %iota_compare_fusion.11, bf16[3,864,4,64]{1,3,2,0:T(8,128)(2,1)} %get-tuple-element.843, s32[]{:T(128)S(6)} %copy.131, ...), kind=kOutput, calls=%fused_computation.84.clone.1 | convolution fusion | flops 397132416 | bytes 25277952 | tf_op jit(solution)/shard_map/while/body/eval_jaxpr/shd,thd->hst/dot_general | solution.py:116
  434.6 6.9 %multiply_convert_fusion.19 = bf16[4,864,864]{1,2,0:T(8,128)(2,1)S(1)} fusion(f32[4,864,864]{1,2,0:T(8,128)} %get-tuple-element.730, f32[4,864,864]{1,2,0:T(8,128)S(1)} %fusion.274, f32[4,864]{1,0:T(4,128)S(1)} %get-tuple-element.731, f32[4,864]{1,0:T(4,128)S(1)} %dynamic-slice_bitcast_fusion.6, pred[864]{0:T(1024)(128)(4,1)S(1)} %iota_compare_fusion.11), kind=kLoop, calls=%fused_computation.83.clone.1 | loop fusion | flops 17915904 | bytes 29888352 | tf_op jit(solution)/shard_map/while/body/eval_jaxpr/convert_element_type | solution.py:121
  448.9 2.9 fusion.277
  451.8 9.5 %multiply_reduce_fusion.16 = (f32[4,864]{1,0:T(4,128)S(1)}, f32[4,864,864]{1,2,0:T(8,128)}) fusion(f32[4,864,864]{1,2,0:T(8,128)S(1)} %fusion.274, f32[4,864]{1,0:T(4,128)S(1)} %dynamic-slice_bitcast_fusion.6, pred[864]{0:T(1024)(128)(4,1)S(1)} %iota_compare_fusion.11, bf16[3,864,4,64]{1,3,2,0:T(8,128)(2,1)} %get-tuple-element.843, s32[]{:T(128)S(6)} %copy.131, ...), kind=kOutput, calls=%fused_computation.84.clone.1 | convolution fusion | flops 397132416 | bytes 25277952 | tf_op jit(solution)/shard_map/while/body/eval_jaxpr/shd,thd->hst/dot_general | solution.py:116
  461.3 6.9 %multiply_convert_fusion.19 = bf16[4,864,864]{1,2,0:T(8,128)(2,1)S(1)} fusion(f32[4,864,864]{1,2,0:T(8,128)} %get-tuple-element.730, f32[4,864,864]{1,2,0:T(8,128)S(1)} %fusion.274, f32[4,864]{1,0:T(4,128)S(1)} %get-tuple-element.731, f32[4,864]{1,0:T(4,128)S(1)} %dynamic-slice_bitcast_fusion.6, pred[864]{0:T(1024)(128)(4,1)S(1)} %iota_compare_fusion.11), kind=kLoop, calls=%fused_computation.83.clone.1 | loop fusion | flops 17915904 | bytes 29888352 | tf_op jit(solution)/shard_map/while/body/eval_jaxpr/convert_element_type | solution.py:121
  472.6 9.2 %fusion.134 = (bf16[768]{0:T(1024)(128)(2,1)S(1)}, f32[864]{0:T(1024)S(1)}, f32[864]{0:T(1024)S(1)}, bf16[768]{0:T(1024)(128)(2,1)S(1)}, f32[864,768]{1,0:T(8,128)}) fusion(bf16[1,864,768]{2,1,0:T(8,128)(2,1)} %param.22, f32[864]{0:T(1024)S(1)} %copy-done.55, f32[864]{0:T(1024)S(1)} %copy-done.46, f32[768]{0:T(1024)S(1)} %copy-done.50, ...), kind=kOutput, calls=%fused_computation.159 | convolution fusion | flops 3076224000 | bytes 11521536 | tf_op jit(solution)/shard_map/dot_general | solution.py:50
  481.9 6.1 convolution_convert_fusion.3
  494.4 3.5 all-to-all-start.1
  497.9 113.3 %reduce_gradients.1 = (f32[48,1152]{1,0:T(8,128)}, f32[48,384]{1,0:T(8,128)}, f32[48,384]{1,0:T(8,128)}, f32[48,768]{1,0:T(8,128)}, f32[48,384]{1,0:T(8,128)}, /*index=5*/f32[48,1536]{1,0:T(8,128)}, f32[192,384]{1,0:T(8,128)}) custom-call(bf16[4,2,2,48,2304]{4,3,2,1,0:T(8,128)(2,1)} %bitcast.387, bf16[4,2,2,48,768]{4,3,2,1,0:T(8,128)(2,1)} %bitcast.401, ...), custom_call_target="tpu_custom_call" | custom-call | tf_op jit(solution)/shard_map/reduce_gradients/pallas_call | solution.py:473
  618.9 3.4 fusion.133
  622.5 33.4 %all-gather = bf16[32,1,1728]{2,1,0:T(2,128)(2,1)S(1)} all-gather(bf16[4,1,1728]{2,1,0:T(2,128)(2,1)S(1)} %reshape.323), channel_id=2, replica_groups=mesh['dp'=8,'fsdp'=4] {'dp'}, dimensions={0}, use_global_device_ids=true | all-gather | bytes 124416 | tf_op jit(solution)/shard_map/all_gather | solution.py:520
  (412 shorter events, 138.3 us)
Async XLA Ops:
  7.2 163.1 %copy-start = (bf16[1,256,768]{2,1,0:T(8,128)(2,1)S(1)}, bf16[1,256,768]{2,1,0:T(8,128)(2,1)}, u32[]{:S(2)}) copy-start(bf16[1,256,768]{2,1,0:T(8,128)(2,1)} %param.23) | copy-start | bytes 1179652
  7.2 51.0 %copy-start.6 = (bf16[1,864,768]{2,1,0:T(8,128)(2,1)S(1)}, bf16[1,864,768]{2,1,0:T(8,128)(2,1)}, u32[]{:S(2)}) copy-start(bf16[1,864,768]{2,1,0:T(8,128)(2,1)} %param.22) | copy-start | bytes 3981316
  7.2 51.8 %copy-start.41 = (bf16[384,192]{0,1:T(8,128)(2,1)S(1)}, bf16[384,192]{0,1:T(8,128)(2,1)}, u32[]{:S(2)}) copy-start(bf16[384,192]{0,1:T(8,128)(2,1)} %param.35) | copy-start | bytes 442372
  7.2 52.0 %copy-start.42 = (bf16[96,768]{1,0:T(8,128)(2,1)S(1)}, bf16[96,768]{1,0:T(8,128)(2,1)}, u32[]{:S(2)}) copy-start(bf16[96,768]{1,0:T(8,128)(2,1)} %param.34) | copy-start | bytes 442372
  7.2 165.6 %all-reduce.4.cloned.1.call-start = ((), (), s32[]{:S(2)}) async-start(), calls=%async_computation.2 | async-start | bytes 458752
  8.2 52.6 %collective-permute-start.1 = (bf16[48,192]{1,0:T(8,128)(2,1)S(1)}, bf16[48,192]{1,0:T(8,128)(2,1)S(1)}, u32[]{:S(2)}, u32[]{:S(2)}) collective-permute-start(bf16[48,192]{1,0:T(8,128)(2,1)S(1)} %get-tuple-element.498), channel_id=1, source_target_pairs={{0,1},{1,0},{2,3},{3,2},{4,5},{5,4},{6,7},{7,6},{8,9},{9,8},{10,11... | collective-permute-start | bytes 55304 | tf_op jit(solution)/shard_map/ppermute | solution.py:180
  9.4 52.2 %collective-permute-start.2 = (bf16[48,192]{1,0:T(8,128)(2,1)S(1)}, bf16[48,192]{1,0:T(8,128)(2,1)S(1)}, u32[]{:S(2)}, u32[]{:S(2)}) collective-permute-start(bf16[48,192]{1,0:T(8,128)(2,1)S(1)} %get-tuple-element.496), channel_id=1, source_target_pairs={{0,1},{1,0},{2,3},{3,2},{4,5},{5,4},{6,7},{7,6},{8,9},{9,8},{10,11... | collective-permute-start | bytes 55304 | tf_op jit(solution)/shard_map/ppermute | solution.py:180
  10.2 49.3 %copy-start.77 = (u32[32]{0:T(128)S(1)}, u32[32]{0:T(128)}, u32[]{:S(2)}) copy-start(u32[32]{0:T(128)} %constant.181) | copy-start | bytes 388
  10.2 52.5 %collective-permute-start.4 = (bf16[48,192]{1,0:T(8,128)(2,1)S(1)}, bf16[48,192]{1,0:T(8,128)(2,1)S(1)}, u32[]{:S(2)}, u32[]{:S(2)}) collective-permute-start(bf16[48,192]{1,0:T(8,128)(2,1)S(1)} %get-tuple-element.494), channel_id=1, source_target_pairs={{0,1},{1,0},{2,3},{3,2},{4,5},{5,4},{6,7},{7,6},{8,9},{9,8},{10,11... | collective-permute-start | bytes 55304 | tf_op jit(solution)/shard_map/ppermute | solution.py:180
  11.5 52.0 %collective-permute-start.3 = (bf16[48,384]{1,0:T(8,128)(2,1)S(1)}, bf16[48,384]{1,0:T(8,128)(2,1)S(1)}, u32[]{:S(2)}, u32[]{:S(2)}) collective-permute-start(bf16[48,384]{1,0:T(8,128)(2,1)S(1)} %get-tuple-element.492), channel_id=1, source_target_pairs={{0,1},{1,0},{2,3},{3,2},{4,5},{5,4},{6,7},{7,6},{8,9},{9,8},{10,11... | collective-permute-start | bytes 110600 | tf_op jit(solution)/shard_map/ppermute | solution.py:180
  12.5 51.7 %collective-permute-start = (bf16[48,576]{1,0:T(8,128)(2,1)S(1)}, bf16[48,576]{1,0:T(8,128)(2,1)S(1)}, u32[]{:S(2)}, u32[]{:S(2)}) collective-permute-start(bf16[48,576]{1,0:T(8,128)(2,1)S(1)} %get-tuple-element.484), channel_id=1, source_target_pairs={{0,1},{1,0},{2,3},{3,2},{4,5},{5,4},{6,7},{7,6},{8,9},{9,8},{10,11... | collective-permute-start | bytes 165896 | tf_op jit(solution)/shard_map/ppermute | solution.py:180
  58.4 124.1 %copy-start.45 = (f32[864]{0:T(1024)}, f32[864]{0:T(1024)S(1)}, u32[]{:S(2)}) copy-start(f32[864]{0:T(1024)S(1)} %broadcast_multiply_fusion.8) | copy-start | bytes 10372
  59.0 123.5 %copy-start.54 = (f32[864]{0:T(1024)}, f32[864]{0:T(1024)S(1)}, u32[]{:S(2)}) copy-start(f32[864]{0:T(1024)S(1)} %add_rsqrt_fusion.2) | copy-start | bytes 10372
  60.8 4.1 collective-permute-start.5
  61.6 4.0 collective-permute-start.6
  174.3 7.4 %all-to-all-start = ((f32[4,1,1728]{2,1,0:T(1,128)}), f32[4,1,1728]{2,1,0:T(1,128)S(1)}, u32[]{:S(2)}, u32[]{:S(2)}) async-start(f32[4,1,1728]{2,1,0:T(1,128)} %copy.65), calls=%async_computation | async-start | bytes 57344 | tf_op jit(solution)/shard_map/all_to_all | solution.py:513
  182.5 57.5 %copy-start.43 = (f32[768]{0:T(1024)}, f32[768]{0:T(1024)S(1)}, u32[]{:S(2)}) copy-start(f32[768]{0:T(1024)S(1)} %get-tuple-element.377) | copy-start | bytes 9220
  182.5 62.9 %copy-start.51 = (f32[768]{0:T(1024)}, f32[768]{0:T(1024)S(1)}, u32[]{:S(2)}) copy-start(f32[768]{0:T(1024)S(1)} %get-tuple-element.373) | copy-start | bytes 9220
  182.5 62.9 %copy-start.61 = (f32[768]{0:T(1024)}, f32[768]{0:T(1024)S(1)}, u32[]{:S(2)}) copy-start(f32[768]{0:T(1024)S(1)} %get-tuple-element.372) | copy-start | bytes 9220
  252.5 20.1 %copy-start.53 = (f32[768]{0:T(1024)S(1)}, f32[768]{0:T(1024)}, u32[]{:S(2)}) copy-start(f32[768]{0:T(1024)} %get-tuple-element.374) | copy-start | bytes 9220
  276.7 19.1 %slice-start = ((s8[4718592]{0:T(1024)(128)(4,1)}), s8[4194304]{0:T(1024)(128)(4,1)S(1)}, s32[]{:S(2)}) async-start(s8[4718592]{0:T(1024)(128)(4,1)} %bitcast.409), calls=%async_computation.3 | async-start | bytes 8388608
  283.9 11.8 %slice-start.1 = ((s8[4718592]{0:T(1024)(128)(4,1)}), s8[524288]{0:T(1024)(128)(4,1)S(1)}, s32[]{:S(2)}) async-start(s8[4718592]{0:T(1024)(128)(4,1)} %bitcast.409), calls=%async_computation.4 | async-start | bytes 1048576
  308.4 9.5 %copy-start.78 = (bf16[864,3072]{1,0:T(8,128)(2,1)S(1)}, bf16[864,3072]{1,0:T(8,128)(2,1)}, u32[]{:S(2)}) copy-start(bf16[864,3072]{1,0:T(8,128)(2,1)} %fusion.117) | copy-start | bytes 15925252
  325.8 11.4 %copy-start.13 = (bf16[3,864,4,64]{1,3,2,0:T(8,128)(2,1)S(1)}, bf16[3,864,4,64]{1,3,2,0:T(8,128)(2,1)}, u32[]{:S(2)}) copy-start(bf16[3,864,4,64]{1,3,2,0:T(8,128)(2,1)} %get-tuple-element.214) | copy-start | bytes 3981316
  345.7 27.9 %copy-start.48 = (f32[864]{0:T(1024)S(1)}, f32[864]{0:T(1024)}, u32[]{:S(2)}) copy-start(f32[864]{0:T(1024)} %copy-done.47) | copy-start | bytes 10372
  345.7 27.9 %copy-start.52 = (f32[768]{0:T(1024)S(1)}, f32[768]{0:T(1024)}, u32[]{:S(2)}) copy-start(f32[768]{0:T(1024)} %copy-done.51) | copy-start | bytes 9220
  345.7 27.9 %copy-start.57 = (f32[864]{0:T(1024)S(1)}, f32[864]{0:T(1024)}, u32[]{:S(2)}) copy-start(f32[864]{0:T(1024)} %copy-done.56) | copy-start | bytes 10372
  345.8 27.9 %copy-start.62 = (f32[768]{0:T(1024)S(1)}, f32[768]{0:T(1024)}, u32[]{:S(2)}) copy-start(f32[768]{0:T(1024)} %copy-done.61) | copy-start | bytes 9220
  391.8 80.8 %copy-start.46 = (f32[864]{0:T(1024)S(1)}, f32[864]{0:T(1024)}, u32[]{:S(2)}) copy-start(f32[864]{0:T(1024)} %copy-done.45) | copy-start | bytes 10372
  391.8 80.8 %copy-start.50 = (f32[768]{0:T(1024)S(1)}, f32[768]{0:T(1024)}, u32[]{:S(2)}) copy-start(f32[768]{0:T(1024)} %copy-done.49) | copy-start | bytes 9220
  391.8 80.8 %copy-start.55 = (f32[864]{0:T(1024)S(1)}, f32[864]{0:T(1024)}, u32[]{:S(2)}) copy-start(f32[864]{0:T(1024)} %copy-done.54) | copy-start | bytes 10372
  398.4 9.5 %copy-start.17 = (bf16[3,864,4,64]{1,3,2,0:T(8,128)(2,1)}, bf16[3,864,4,64]{1,3,2,0:T(8,128)(2,1)S(1)}, u32[]{:S(2)}) copy-start(bf16[3,864,4,64]{1,3,2,0:T(8,128)(2,1)S(1)} %fusion.277) | copy-start | bytes 3981316 | tf_op jit(solution)/shard_map/while
  425.1 9.5 %copy-start.17 = (bf16[3,864,4,64]{1,3,2,0:T(8,128)(2,1)}, bf16[3,864,4,64]{1,3,2,0:T(8,128)(2,1)S(1)}, u32[]{:S(2)}) copy-start(bf16[3,864,4,64]{1,3,2,0:T(8,128)(2,1)S(1)} %fusion.277) | copy-start | bytes 3981316 | tf_op jit(solution)/shard_map/while
  451.8 9.5 %copy-start.17 = (bf16[3,864,4,64]{1,3,2,0:T(8,128)(2,1)}, bf16[3,864,4,64]{1,3,2,0:T(8,128)(2,1)S(1)}, u32[]{:S(2)}) copy-start(bf16[3,864,4,64]{1,3,2,0:T(8,128)(2,1)S(1)} %fusion.277) | copy-start | bytes 3981316 | tf_op jit(solution)/shard_map/while
  472.6 9.3 %copy-start.7 = (bf16[1,864,768]{2,1,0:T(8,128)(2,1)S(1)}, bf16[1,864,768]{2,1,0:T(8,128)(2,1)}, u32[]{:S(2)}) copy-start(bf16[1,864,768]{2,1,0:T(8,128)(2,1)} %param.22) | copy-start | bytes 3981316
  472.6 9.3 %copy-start.18 = (bf16[3,864,4,64]{1,3,2,0:T(8,128)(2,1)S(1)}, bf16[3,864,4,64]{1,3,2,0:T(8,128)(2,1)}, u32[]{:S(2)}) copy-start(bf16[3,864,4,64]{1,3,2,0:T(8,128)(2,1)} %get-tuple-element.223) | copy-start | bytes 3981316
  472.6 9.3 %copy-start.21 = (bf16[3,864,4,64]{1,3,2,0:T(8,128)(2,1)S(1)}, bf16[3,864,4,64]{1,3,2,0:T(8,128)(2,1)}, u32[]{:S(2)}) copy-start(bf16[3,864,4,64]{1,3,2,0:T(8,128)(2,1)} %get-tuple-element.222) | copy-start | bytes 3981316
  494.4 128.0 %all-to-all-start.1 = ((bf16[4,2,864]{2,1,0:T(2,128)(2,1)}), bf16[4,2,864]{2,1,0:T(2,128)(2,1)S(1)}, u32[]{:S(2)}, u32[]{:S(2)}) async-start(bf16[4,2,864]{2,1,0:T(2,128)(2,1)} %reshape.322), calls=%async_computation.1 | async-start | bytes 28672 | tf_op jit(solution)/shard_map/all_to_all | solution.py:519
  497.8 121.1 %copy-start.10 = (f32[864,768]{1,0:T(8,128)S(1)}, f32[864,768]{1,0:T(8,128)}, u32[]{:S(2)}) copy-start(f32[864,768]{1,0:T(8,128)} %copy-done.9) | copy-start | bytes 7962628
  612.2 44.9 %collective-permute-start.8 = (f32[48,192]{1,0:T(8,128)S(1)}, f32[48,192]{1,0:T(8,128)S(1)}, u32[]{:S(2)}, u32[]{:S(2)}) collective-permute-start(f32[48,192]{1,0:T(8,128)S(1)} %get-tuple-element.490), channel_id=1, source_target_pairs={{0,1},{1,0},{2,3},{3,2},{4,5},{5,4},{6,7},{7,6},{8,9},{9,8},{10,11... | collective-permute-start | bytes 110600 | tf_op jit(solution)/shard_map/ppermute | solution.py:180
  613.2 44.5 %collective-permute-start.9 = (f32[48,192]{1,0:T(8,128)S(1)}, f32[48,192]{1,0:T(8,128)S(1)}, u32[]{:S(2)}, u32[]{:S(2)}) collective-permute-start(f32[48,192]{1,0:T(8,128)S(1)} %get-tuple-element.488), channel_id=1, source_target_pairs={{0,1},{1,0},{2,3},{3,2},{4,5},{5,4},{6,7},{7,6},{8,9},{9,8},{10,11... | collective-permute-start | bytes 110600 | tf_op jit(solution)/shard_map/ppermute | solution.py:180
  614.9 44.1 %collective-permute-start.11 = (f32[48,192]{1,0:T(8,128)S(1)}, f32[48,192]{1,0:T(8,128)S(1)}, u32[]{:S(2)}, u32[]{:S(2)}) collective-permute-start(f32[48,192]{1,0:T(8,128)S(1)} %get-tuple-element.486), channel_id=1, source_target_pairs={{0,1},{1,0},{2,3},{3,2},{4,5},{5,4},{6,7},{7,6},{8,9},{9,8},{10,11... | collective-permute-start | bytes 110600 | tf_op jit(solution)/shard_map/ppermute | solution.py:180
  617.3 42.9 %collective-permute-start.7 = (f32[48,576]{1,0:T(8,128)S(1)}, f32[48,576]{1,0:T(8,128)S(1)}, u32[]{:S(2)}, u32[]{:S(2)}) collective-permute-start(f32[48,576]{1,0:T(8,128)S(1)} %get-tuple-element.476), channel_id=1, source_target_pairs={{0,1},{1,0},{2,3},{3,2},{4,5},{5,4},{6,7},{7,6},{8,9},{9,8},{10,11... | collective-permute-start | bytes 331784 | tf_op jit(solution)/shard_map/ppermute | solution.py:180
  618.8 40.8 %collective-permute-start.10 = (f32[48,384]{1,0:T(8,128)S(1)}, f32[48,384]{1,0:T(8,128)S(1)}, u32[]{:S(2)}, u32[]{:S(2)}) collective-permute-start(f32[48,384]{1,0:T(8,128)S(1)} %get-tuple-element.478), channel_id=1, source_target_pairs={{0,1},{1,0},{2,3},{3,2},{4,5},{5,4},{6,7},{7,6},{8,9},{9,8},{10,11... | collective-permute-start | bytes 221192 | tf_op jit(solution)/shard_map/ppermute | solution.py:180
  618.9 37.0 %copy-start.31 = (f32[32,384]{1,0:T(8,128)S(1)}, f32[32,384]{1,0:T(8,128)}, u32[]{:S(2)}) copy-start(f32[32,384]{1,0:T(8,128)} %copy-done.30) | copy-start | bytes 147460
  618.9 37.0 %copy-start.33 = (f32[32,384]{1,0:T(8,128)S(1)}, f32[32,384]{1,0:T(8,128)}, u32[]{:S(2)}) copy-start(f32[32,384]{1,0:T(8,128)} %copy-done.32) | copy-start | bytes 147460
  657.1 3.9 collective-permute-start.13
  657.7 4.1 collective-permute-start.12
  (81 other events, 233.5 us)
Sparse Core Ops, SparseCore 0:
  58.3 82.5 all-reduce.3

commit v2 on v1

--- a/solution.py
+++ b/solution.py
@@ -44,108 +44,6 @@
     return lax.dot_general(
         left, right, (((0,), (0,)), ((), ())), preferred_element_type=jnp.float32
     )
-
-
-def through(gradient, matrix):
-    return lax.dot_general(
-        gradient, matrix, (((1,), (1,)), ((), ())), preferred_element_type=jnp.float32
-    )
-
-
-def gelu_tanh(values):
-    return jax.nn.gelu(values, approximate=True)
-
-
-def group_count(head_count):
-    return head_count // 4
-
-
-def split_groups(array, groups):
-    rows, head_count, head_size = array.shape
-    return jnp.moveaxis(array.reshape(rows, groups, head_count // groups, head_size), 1, 0)
-
-
-def join_groups(array):
-    return jnp.moveaxis(array, 0, 1).reshape(array.shape[1], -1)
-
-
-def attend_forward(query_rows, key_rows, value_rows, key_valid):
-    factor = query_rows.shape[-1] ** (-0.5)
-    groups = group_count(query_rows.shape[1])
-
-    def one_group(packed):
-        query_part, key_part, value_part = packed
-        scores = (
-            jnp.einsum("shd,thd->hst", query_part, key_part, preferred_element_type=jnp.float32)
-            * factor
-        )
-        scores = jnp.where(key_valid[None, None, :], scores, -1e30)
-        largest = jnp.max(scores, -1, keepdims=True)
-        exponent = jnp.exp(scores - largest)
-        summed = jnp.sum(exponent, -1, keepdims=True)
-        shares = (exponent / summed).astype(jnp.bfloat16)
-        mixed_part = jnp.einsum(
-            "hst,thd->shd", shares, value_part, preferred_element_type=jnp.float32
-        )
-        return (mixed_part.astype(jnp.bfloat16), (largest + jnp.log(summed))[..., 0])
-
-    mixed_heads, log_total = lax.map(
-        one_group,
-        (
-            split_groups(query_rows, groups),
-            split_groups(key_rows, groups),
-            split_groups(value_rows, groups),
-        ),
-    )
-    return (join_groups(mixed_heads), log_total)
-
-
-def attend_back(query_rows, key_rows, value_rows, key_valid, log_total, upstream):
-    factor = query_rows.shape[-1] ** (-0.5)
-    groups = group_count(query_rows.shape[1])
-    upstream_heads = upstream.reshape(query_rows.shape)
-
-    def one_group(packed):
-        query_part, key_part, value_part, log_part, upstream_part = packed
-        scores = (
-            jnp.einsum("shd,thd->hst", query_part, key_part, preferred_element_type=jnp.float32)
-            * factor
-        )
-        scores = jnp.where(key_valid[None, None, :], scores, -1e30)
-        shares = jnp.exp(scores - log_part[..., None])
-        share_grad = jnp.einsum(
-            "shd,thd->hst", upstream_part, value_part, preferred_element_type=jnp.float32
-        )
-        score_grad = (
-            shares * (share_grad - jnp.sum(shares * share_grad, -1, keepdims=True))
-        ).astype(jnp.bfloat16)
-        query_grad = (
-            jnp.einsum("hst,thd->shd", score_grad, key_part, preferred_element_type=jnp.float32)
-            * factor
-        )
-        key_grad = (
-            jnp.einsum("hst,shd->thd", score_grad, query_part, preferred_element_type=jnp.float32)
-            * factor
-        )
-        value_grad = jnp.einsum(
-            "hst,shd->thd",
-            shares.astype(jnp.bfloat16),
-            upstream_part,
-            preferred_element_type=jnp.float32,
-        )
-        return (query_grad, key_grad, value_grad)
-
-    query_grad, key_grad, value_grad = lax.map(
-        one_group,
-        (
-            split_groups(query_rows, groups),
-            split_groups(key_rows, groups),
-            split_groups(value_rows, groups),
-            log_total,
-            split_groups(upstream_heads, groups),
-        ),
-    )
-    return (join_groups(query_grad), join_groups(key_grad), join_groups(value_grad))
 
 
 MESH = pl.DeviceIdType.MESH
@@ -281,7 +179,9 @@
 def gather_weights(grid, matrices):
     if not grid.fits(matrices):
         return tuple(
-            lax.all_gather(lax.all_gather(m, "fsdp", axis=1, tiled=True), "dp", axis=0, tiled=True)
+            lax.all_gather(
+                lax.all_gather(m, "fsdp", axis=1, tiled=True), "dp", axis=0, tiled=True
+            ).reshape(4, 2, 2, m.shape[0] * grid.dp // 16, m.shape[1] * grid.fsdp)
             for m in matrices
         )
     core = lax.axis_index("fsdp") % 2
@@ -313,7 +213,7 @@
         compiler_params=pltpu.CompilerParams(collective_id=0, has_side_effects=True),
         name="gather_weights",
     )(*blocks)
-    return tuple(w.reshape(-1, w.shape[-1]) for w in wholes)
+    return tuple(wholes)
 
 
 def reduce_kernel(nz, count, *refs):
@@ -442,10 +342,10 @@
 
 
 def reduce_gradients(grid, gradients):
-    rounded = [g.astype(jnp.bfloat16) for g in gradients]
+    rounded = [g.reshape(-1, g.shape[-1]) for g in gradients]
     blocks = [
         jax.ShapeDtypeStruct((g.shape[0] // grid.dp, g.shape[1] // grid.fsdp), jnp.bfloat16)
-        for g in gradients
+        for g in rounded
     ]
     if not grid.fits(blocks):
         out = []
@@ -456,7 +356,7 @@
         return tuple(out)
     nz = grid.nz
     count = len(rounded)
-    shaped = [g.reshape(nz, 2, 2, g.shape[0] // (nz * 4), g.shape[1]) for g in rounded]
+    shaped = list(gradients)
     rows = [g.shape[3] for g in shaped]
     widths = [g.shape[4] for g in shaped]
     bf16 = jnp.bfloat16
@@ -521,6 +421,486 @@
     return outer_sum(conditions, everyone)
 
 
+F32 = jnp.float32
+BF16 = jnp.bfloat16
+NT = (((1,), (1,)), ((), ()))
+TN = (((0,), (0,)), ((), ()))
+
+
+def flat(value):
+    return value.reshape(-1, value.shape[-1])
+
+
+def dot(left, right):
+    return jnp.dot(left, right, preferred_element_type=F32)
+
+
+def dot_nt(left, right):
+    return lax.dot_general(left, right, NT, preferred_element_type=F32)
+
+
+def dot_tn(left, right):
+    return lax.dot_general(left, right, TN, preferred_element_type=F32)
+
+
+def tiles(total, size, body):
+    def step(t, carry):
+        body(pl.ds(pl.multiple_of(t * size, size), size))
+        return carry
+
+    lax.fori_loop(0, total // size, step, 0)
+
+
+def row_tile(rows):
+    for size in (432, 288, 256, 128):
+        if rows % size == 0:
+            return size
+    return rows
+
+
+def gelu_pair(inner):
+    slope = math.sqrt(2.0 / math.pi)
+    square = inner * inner
+    turned = jnp.tanh(inner * (slope + (slope * 0.044715) * square))
+    half = 0.5 + 0.5 * turned
+    rise = inner * (slope + (3.0 * slope * 0.044715) * square)
+    return inner * half, half + (0.5 - 0.5 * turned * turned) * rise
+
+
+def half_lanes(shape):
+    return lax.broadcasted_iota(jnp.int32, shape, 1) < shape[1] // 2
+
+
+def attend(queries, keys, values, bias, mixed, heads_wide, size):
+    query_ref, query_at = queries
+    key_ref, key_at = keys
+    value_ref, value_at = values
+    mixed_ref, mixed_at = mixed
+    rows = mixed_ref.shape[0]
+    width = 2 * heads_wide
+
+    def pair(p, carry):
+        def at(start):
+            return pl.ds(pl.multiple_of(start + p * width, width), width)
+
+        key_pair = key_ref[:, at(key_at)]
+        value_pair = value_ref[:, at(value_at)]
+        low = half_lanes((size, width))
+        for start in range(0, rows, size):
+            scaled = query_ref[start : start + size, at(query_at)] * BF16(heads_wide**-0.5)
+            outs = []
+            for head in range(2):
+                own = jnp.where(low if head == 0 else ~low, scaled, BF16(0))
+                scores = dot_nt(own, key_pair) + bias[...]
+                raised = jnp.exp(scores - jnp.max(scores, -1, keepdims=True))
+                summed = jnp.sum(raised, -1, keepdims=True)
+                outs.append(dot(raised.astype(BF16), value_pair) * (1.0 / summed))
+            mixed_ref[start : start + size, at(mixed_at)] = jnp.where(
+                low, outs[0], outs[1]
+            ).astype(BF16)
+        return carry
+
+    return pair
+
+
+def attend_back(queries, keys, values, bias, upstream, heads_wide, size):
+    query_ref, query_at = queries
+    key_ref, key_at = keys
+    value_ref, value_at = values
+    rows = upstream.shape[0]
+    slots = bias.shape[1]
+    width = 2 * heads_wide
+    factor = BF16(heads_wide**-0.5)
+
+    def pair(p, carry):
+        def at(start):
+            return pl.ds(pl.multiple_of(start + p * width, width), width)
+
+        key_pair = key_ref[:, at(key_at)]
+        value_pair = value_ref[:, at(value_at)]
+        low = half_lanes((size, width))
+        low_keys = half_lanes((slots, width))
+        key_grad = jnp.zeros((slots, width), F32)
+        value_grad = jnp.zeros((slots, width), F32)
+        for start in range(0, rows, size):
+            scaled = query_ref[start : start + size, at(query_at)] * factor
+            above = upstream[start : start + size, at(0)]
+            query_grad = jnp.zeros((size, width), F32)
+            for head in range(2):
+                mask = low if head == 0 else ~low
+                own = jnp.where(mask, scaled, BF16(0))
+                own_above = jnp.where(mask, above, BF16(0))
+                own_keys = jnp.where(low_keys if head == 0 else ~low_keys, key_pair, BF16(0))
+                scores = dot_nt(own, key_pair) + bias[...]
+                raised = jnp.exp(scores - jnp.max(scores, -1, keepdims=True))
+                shares = raised * (1.0 / jnp.sum(raised, -1, keepdims=True))
+                share_grad = dot_nt(own_above, value_pair)
+                total = jnp.sum(shares * share_grad, -1, keepdims=True)
+                score_grad = (shares * (share_grad - total)).astype(BF16)
+                value_grad += dot_tn(shares.astype(BF16), own_above)
+                key_grad += dot_tn(score_grad, own)
+                query_grad += dot(score_grad, own_keys)
+            query_ref[start : start + size, at(query_at)] = (
+                query_grad * heads_wide**-0.5
+            ).astype(BF16)
+        key_ref[:, at(key_at)] = key_grad.astype(BF16)
+        value_ref[:, at(value_at)] = value_grad.astype(BF16)
+        return carry
+
+    return pair
+
+
+class Loads:
+    def __init__(self, sems):
+        self.sems = sems
+        self.copies = {}
+
+    def start(self, name, src, dst):
+        copy = pltpu.make_async_copy(src, dst, self.sems.at[len(self.copies)])
+        copy.start()
+        self.copies[name] = copy
+
+    def wait(self, *names):
+        for name in names:
+            self.copies[name].wait()
+
+
+WEIGHTS = ("qkv", "out", "cq", "ckv", "cout", "fc1", "fc2")
+
+
+def forward_kernel(*refs):
+    (lat, text, og, mod, frame_bias, text_bias), refs = refs[:6], refs[6:]
+    given, refs = dict(zip(WEIGHTS, refs[:7])), refs[7:]
+    (layer_out, dcross_out, qkv_out, h1_out, mixed1_out, h2_out, q2_out, mixed2_out), refs = (
+        refs[:8],
+        refs[8:],
+    )
+    (memory_out, after_out, branch_out, fc1_out, fc2_out, rows_out), refs = refs[:6], refs[6:]
+    held, refs = dict(zip(WEIGHTS, refs[:7])), refs[7:]
+    big, wide, h3, db3, memory, after_self, branch_1, branch_2, after_cross, result, sems = refs
+    slots, model = lat.shape
+    inner_width = held["fc1"].shape[-1]
+    head = model // HEADS
+    size = row_tile(slots)
+    loads = Loads(sems)
+    for name in WEIGHTS:
+        loads.start(name, given[name], held[name])
+
+    def need(name):
+        loads.wait(name)
+
+    def row(k):
+        return mod[k : k + 1, :]
+
+    big[slots:, :] = jnp.zeros((big.shape[0] - slots, inner_width), BF16)
+
+    def norm_1(rows):
+        normed, _ = normalize(lat[rows, :].astype(F32))
+        wide[rows, 0:model] = (normed * (1.0 + row(1)) + row(0)).astype(BF16)
+
+    tiles(slots, size, norm_1)
+    need("qkv")
+    for part in range(3):
+        columns = slice(part * model, (part + 1) * model)
+
+        def project(rows):
+            big[rows, columns] = dot(
+                wide[rows, 0:model], flat(held["qkv"][:, :, :, :, columns])
+            ).astype(BF16)
+
+        tiles(slots, size, project)
+    loads.start("qkv_out", big.at[0:slots, 0 : 3 * model], qkv_out)
+    loads.start("h1_out", wide.at[:, 0:model], h1_out)
+    pair = attend(
+        (big, 0), (big, model), (big, 2 * model), frame_bias, (wide, model), head, size
+    )
+    lax.fori_loop(0, HEADS // 2, pair, 0)
+    loads.start("mixed1_out", wide.at[:, model : 2 * model], mixed1_out)
+    need("out")
+    need("cq")
+
+    def join_1(rows):
+        branch = dot(wide[rows, model : 2 * model], flat(held["out"][...]))
+        branch_1[rows, :] = branch
+        after = lat[rows, :].astype(F32) + row(2) * branch
+        after_self[rows, :] = after
+        normed, _ = normalize(after)
+        hidden = (normed * (1.0 + row(4)) + row(3)).astype(BF16)
+        wide[rows, 2 * model : 3 * model] = hidden
+        wide[rows, 3 * model : 4 * model] = dot(hidden, flat(held["cq"][...])).astype(BF16)
+
+    tiles(slots, size, join_1)
+    loads.start("branch_out", branch_1, branch_out)
+    loads.start("after_out", after_self, after_out)
+    loads.start("h2_out", wide.at[:, 2 * model : 3 * model], h2_out)
+    loads.start("q2_out", wide.at[:, 3 * model : 4 * model], q2_out)
+    need("ckv")
+    for part in range(2):
+        columns = slice(part * model, (part + 1) * model)
+        memory[:, columns] = dot(text[...], flat(held["ckv"][:, :, :, :, columns])).astype(BF16)
+    loads.start("memory_out", memory, memory_out)
+    mixed2 = big.at[0:slots, 3 * model : 4 * model]
+    pair = attend(
+        (wide, 3 * model), (memory, 0), (memory, model), text_bias, (mixed2, 0), head, size
+    )
+    lax.fori_loop(0, HEADS // 2, pair, 0)
+    loads.start("mixed2_out", mixed2, mixed2_out)
+    need("cout")
+
+    def join_2(rows):
+        branch = dot(mixed2[rows, :], flat(held["cout"][...]))
+        branch_2[rows, :] = branch
+        after = after_self[rows, :] + row(5) * branch
+        after_cross[rows, :] = after
+        normed, _ = normalize(after)
+        h3[rows, :] = (normed * (1.0 + row(7)) + row(6)).astype(BF16)
+        db3[rows, :] = (row(8) * og[rows, :].astype(F32)).astype(BF16)
+
+    tiles(slots, size, join_2)
+    need("fc1")
+    need("fc2")
+    loads.wait("qkv_out", "h1_out", "mixed1_out", "h2_out", "q2_out", "mixed2_out")
+    rows_out[...] = jnp.zeros_like(rows_out)
+    fc2_lead = held["fc2"].shape[0] * held["fc2"].shape[1]
+
+    def feed(rows):
+        hidden = h3[rows, :]
+        above = db3[rows, :]
+        for part in range(inner_width // model):
+            columns = slice(part * model, (part + 1) * model)
+            matrix_1 = flat(held["fc1"][:, :, :, :, columns])
+            per = held["fc2"].shape[0] // (inner_width // model)
+            matrix_2 = flat(held["fc2"][part * per : (part + 1) * per])
+            activated, slope = gelu_pair(dot(hidden, matrix_1))
+            activated = activated.astype(BF16)
+            dinner = (dot_nt(above, matrix_2) * slope).astype(BF16)
+            big[rows, columns] = activated
+            wide[rows, columns] = dinner
+            forward = dot(activated, matrix_2)
+            backward = dot_nt(dinner, matrix_1)
+            if part == 0:
+                branch, upstream = forward, backward
+            else:
+                branch += forward
+                upstream += backward
+        entering = after_cross[rows, :]
+        grad = og[rows, :].astype(F32)
+        result[rows, :] = entering + row(8) * branch
+        normed, inverse = normalize(entering)
+        back, dshift, dscale = norm_back(upstream, normed, inverse, row(7))
+        dcross = grad + back
+        after_cross[rows, :] = dcross
+        rows_out[0:1, :] += jnp.sum(grad * branch, 0, keepdims=True)
+        rows_out[1:2, :] += dshift[None]
+        rows_out[2:3, :] += dscale[None]
+        rows_out[3:4, :] += jnp.sum(dcross * branch_2[rows, :], 0, keepdims=True)
+
+    tiles(slots, size, feed)
+    loads.start("layer_out", result, layer_out)
+    loads.start("dcross_out", after_cross, dcross_out)
+    second = held["fc2"]
+
+    def grad_2(t, carry):
+        a, b = t // second.shape[1], t % second.shape[1]
+        count = inner_width // fc2_lead
+        columns = pl.ds(pl.multiple_of(t * count, 128), count)
+        product = dot_tn(big[0:slots, columns], db3[...]).astype(BF16)
+        second[a, b] = product.reshape(second.shape[2:])
+        return carry
+
+    lax.fori_loop(0, fc2_lead, grad_2, 0)
+    loads.start("fc2_out", second, fc2_out)
+
+    def grad_1(columns):
+        product = dot_tn(h3[...], wide[:, columns]).astype(BF16)
+        held["fc1"][:, :, :, :, columns] = product.reshape(held["fc1"].shape[:4] + (-1,))
+
+    tiles(inner_width, 512, grad_1)
+    loads.start("fc1_out", held["fc1"], fc1_out)
+    loads.wait("branch_out", "after_out", "memory_out", "layer_out", "dcross_out", "fc1_out")
+    loads.wait("fc2_out")
+
+
+def forward(latent, text_block, upstream, modulation, frame_bias, text_bias, matrices):
+    slots, model = latent.shape
+    text_slots = text_block.shape[0]
+    padded = frame_bias.shape[1]
+    inner_width = matrices[5].shape[-1]
+    shaped = jax.ShapeDtypeStruct
+    narrow = shaped((slots, model), BF16)
+    full = shaped((slots, model), F32)
+    outs = [
+        full,
+        full,
+        shaped((slots, 3 * model), BF16),
+        narrow,
+        narrow,
+        narrow,
+        narrow,
+        narrow,
+        shaped((text_slots, 2 * model), BF16),
+        full,
+        full,
+        shaped(matrices[5].shape, BF16),
+        shaped(matrices[6].shape, BF16),
+        shaped((8, model), F32),
+    ]
+    vmem = pl.BlockSpec(memory_space=pltpu.VMEM)
+    anywhere = pl.BlockSpec(memory_space=pl.ANY)
+    scratch = [pltpu.VMEM(m.shape, BF16) for m in matrices]
+    scratch += [
+        pltpu.VMEM((padded, inner_width), BF16),
+        pltpu.VMEM((slots, inner_width), BF16),
+        pltpu.VMEM((slots, model), BF16),
+        pltpu.VMEM((slots, model), BF16),
+        pltpu.VMEM((text_slots, 2 * model), BF16),
+    ]
+    scratch += [pltpu.VMEM((slots, model), F32)] * 5
+    scratch += [pltpu.SemaphoreType.DMA((24,))]
+    return pl.pallas_call(
+        forward_kernel,
+        out_shape=outs,
+        in_specs=[vmem] * 6 + [anywhere] * 7,
+        out_specs=[anywhere] * 13 + [vmem],
+        scratch_shapes=scratch,
+        compiler_params=pltpu.CompilerParams(vmem_limit_bytes=62 * 1024 * 1024),
+        name="forward",
+    )(latent, text_block, upstream, modulation, frame_bias, text_bias, *matrices)
+
+
+BACK = ("qkv", "out", "cq", "ckv", "cout")
+
+
+def backward_kernel(*refs):
+    (lat, text, mod, frame_bias, text_bias), refs = refs[:5], refs[5:]
+    names = ("dcross", "qkv_act", "h1", "mixed1", "h2", "q2", "mixed2", "memory", "after", "branch")
+    given, refs = dict(zip(names, refs[:10])), refs[10:]
+    matrices, refs = dict(zip(BACK, refs[:5])), refs[5:]
+    (latent_out, text_out, rows_out), refs = refs[:3], refs[3:]
+    grads_out, refs = dict(zip(BACK, refs[:5])), refs[5:]
+    act, refs = dict(zip(names, refs[:10])), refs[10:]
+    held, refs = dict(zip(BACK, refs[:5])), refs[5:]
+    grad_qkv, above, sems = refs
+    slots, model = lat.shape
+    head = model // HEADS
+    size = row_tile(slots)
+    loads = Loads(sems)
+    for name in ("dcross", "mixed2", "q2", "memory", "h2", "after", "branch", "mixed1", "h1"):
+        loads.start(name, given[name], act[name])
+    loads.start("qkv_act", given["qkv_act"], act["qkv_act"].at[0:slots, :])
+    for name in ("cout", "cq", "ckv", "out", "qkv"):
+        loads.start("w" + name, matrices[name], held[name])
+
+    def row(k):
+        return mod[k : k + 1, :]
+
+    def place_grad(target, name, columns, left, right):
+        product = dot_tn(left, right).astype(BF16)
+        target[:, :, :, :, columns] = product.reshape(target.shape[:4] + (-1,))
+
+    rows_out[...] = jnp.zeros_like(rows_out)
+    dcross = act["dcross"]
+    loads.wait("dcross", "wcout")
+
+    def enter_2(rows):
+        small = (row(5) * dcross[rows, :]).astype(BF16)
+        above[0, rows, :] = small
+        above[1, rows, :] = dot_nt(small, flat(held["cout"][...])).astype(BF16)
+
+    tiles(slots, size, enter_2)
+    loads.wait("mixed2")
+    place_grad(held["cout"], "cout", slice(0, model), act["mixed2"][...], above[0])
+    loads.start("gcout", held["cout"], grads_out["cout"])
+    loads.wait("q2", "memory")
+    pair = attend_back(
+        (act["q2"], 0), (act["memory"], 0), (act["memory"], model), text_bias, above.at[1], head, size
+    )
+    lax.fori_loop(0, HEADS // 2, pair, 0)
+    loads.wait("wcq", "wckv", "after", "branch", "h2")
+    text_out[...] = dot_nt(act["memory"][...], flat(held["ckv"][...]))
+    for part in range(2):
+        columns = slice(part * model, (part + 1) * model)
+        place_grad(held["ckv"], "ckv", columns, text[...], act["memory"][:, columns])
+    loads.start("gckv", held["ckv"], grads_out["ckv"])
+    loads.wait("wout")
+
+    def leave_2(rows):
+        upstream = dot_nt(act["q2"][rows, :], flat(held["cq"][...]))
+        normed, inverse = normalize(act["after"][rows, :])
+        back, dshift, dscale = norm_back(upstream, normed, inverse, row(4))
+        dself = dcross[rows, :] + back
+        dcross[rows, :] = dself
+        rows_out[0:1, :] += dshift[None]
+        rows_out[1:2, :] += dscale[None]
+        rows_out[2:3, :] += jnp.sum(dself * act["branch"][rows, :], 0, keepdims=True)
+        small = (row(2) * dself).astype(BF16)
+        above[0, rows, :] = small
+        above[1, rows, :] = dot_nt(small, flat(held["out"][...])).astype(BF16)
+
+    tiles(slots, size, leave_2)
+    place_grad(held["cq"], "cq", slice(0, model), act["h2"][...], act["q2"][...])
+    loads.start("gcq", held["cq"], grads_out["cq"])
+    loads.wait("mixed1")
+    place_grad(held["out"], "out", slice(0, model), act["mixed1"][...], above[0])
+    loads.start("gout", held["out"], grads_out["out"])
+    loads.wait("qkv_act")
+    packed = act["qkv_act"]
+    packed[slots:, :] = jnp.zeros((packed.shape[0] - slots, 3 * model), BF16)
+    pair = attend_back(
+        (packed, 0), (packed, model), (packed, 2 * model), frame_bias, above.at[1], head, 288
+    )
+    lax.fori_loop(0, HEADS // 2, pair, 0)
+    loads.wait("h1", "wqkv")
+    for part in range(3):
+        columns = slice(part * model, (part + 1) * model)
+        place_grad(grad_qkv, "qkv", columns, act["h1"][...], packed[0:slots, columns])
+    loads.start("gqkv", grad_qkv, grads_out["qkv"])
+
+    def leave_1(rows):
+        upstream = dot_nt(packed[rows, :], flat(held["qkv"][...]))
+        normed, inverse = normalize(lat[rows, :].astype(F32))
+        back, dshift, dscale = norm_back(upstream, normed, inverse, row(1))
+        dcross[rows, :] = dcross[rows, :] + back
+        rows_out[3:4, :] += dshift[None]
+        rows_out[4:5, :] += dscale[None]
+
+    tiles(slots, size, leave_1)
+    loads.start("latent", dcross, latent_out)
+    loads.wait("gcout", "gckv", "gcq", "gout", "gqkv", "latent")
+
+
+def backward(latent, text_block, modulation, frame_bias, text_bias, kept, matrices):
+    slots, model = latent.shape
+    text_slots = text_block.shape[0]
+    padded = frame_bias.shape[1]
+    shaped = jax.ShapeDtypeStruct
+    outs = [
+        shaped((slots, model), F32),
+        shaped((text_slots, model), F32),
+        shaped((8, model), F32),
+    ]
+    outs += [shaped(m.shape, BF16) for m in matrices]
+    vmem = pl.BlockSpec(memory_space=pltpu.VMEM)
+    anywhere = pl.BlockSpec(memory_space=pl.ANY)
+    scratch = [pltpu.VMEM(k.shape, k.dtype) for k in kept]
+    scratch[1] = pltpu.VMEM((padded, 3 * model), BF16)
+    scratch += [pltpu.VMEM(m.shape, BF16) for m in matrices]
+    scratch += [
+        pltpu.VMEM(matrices[0].shape, BF16),
+        pltpu.VMEM((2, slots, model), BF16),
+        pltpu.SemaphoreType.DMA((24,)),
+    ]
+    return pl.pallas_call(
+        backward_kernel,
+        out_shape=outs,
+        in_specs=[vmem] * 5 + [anywhere] * 15,
+        out_specs=[anywhere, vmem, vmem] + [anywhere] * 5,
+        scratch_shapes=scratch,
+        compiler_params=pltpu.CompilerParams(vmem_limit_bytes=62 * 1024 * 1024),
+        name="backward",
+    )(latent, text_block, modulation, frame_bias, text_bias, *kept, *matrices)
+
+
 def body(
     latents,
     text_rows,
@@ -541,154 +921,53 @@
     fsdp_size,
 ):
     grid = Grid(dp_size, fsdp_size)
-    matrices = (w_qkv, w_out, w_cq, w_ckv, w_cout, w_fc1, w_fc2)
-    full_qkv, full_out, full_cq, full_ckv, full_cout, full_fc1, full_fc2 = gather_weights(
-        grid, matrices
-    )
+    matrices = gather_weights(grid, (w_qkv, w_out, w_cq, w_ckv, w_cout, w_fc1, w_fc2))
     conditions, modulation = modulate(grid, timestep, w_ada)
-    latent = latents[0].astype(jnp.float32)
-    text_block = text_rows[0]
-    slot_count = latent.shape[0]
-    model_width = latent.shape[1]
-    text_slots = text_block.shape[0]
-    head_size = model_width // HEADS
-    frame_valid = jnp.arange(slot_count) < frame_len[0]
-    text_valid = jnp.arange(text_slots) < text_len[0]
-    normed_one, inverse_one = normalize(latent)
-    hidden_one = (normed_one * (1.0 + modulation[1]) + modulation[0]).astype(jnp.bfloat16)
-    packed = jnp.dot(hidden_one, full_qkv, preferred_element_type=jnp.float32).astype(jnp.bfloat16)
-    packed = packed.reshape(slot_count, 3, HEADS, head_size)
-    mixed_one, log_one = attend_forward(packed[:, 0], packed[:, 1], packed[:, 2], frame_valid)
-    branch_one = jnp.dot(mixed_one, full_out, preferred_element_type=jnp.float32)
-    after_self = latent + modulation[2] * branch_one
-    normed_two, inverse_two = normalize(after_self)
-    hidden_two = (normed_two * (1.0 + modulation[4]) + modulation[3]).astype(jnp.bfloat16)
-    query_two = jnp.dot(hidden_two, full_cq, preferred_element_type=jnp.float32).astype(
-        jnp.bfloat16
-    )
-    query_two = query_two.reshape(slot_count, HEADS, head_size)
-    memory = jnp.dot(text_block, full_ckv, preferred_element_type=jnp.float32).astype(jnp.bfloat16)
-    memory = memory.reshape(text_slots, 2, HEADS, head_size)
-    mixed_two, log_two = attend_forward(query_two, memory[:, 0], memory[:, 1], text_valid)
-    branch_two = jnp.dot(mixed_two, full_cout, preferred_element_type=jnp.float32)
-    after_cross = after_self + modulation[5] * branch_two
-    normed_three, inverse_three = normalize(after_cross)
-    hidden_three = (normed_three * (1.0 + modulation[7]) + modulation[6]).astype(jnp.bfloat16)
-    pre_gelu = jnp.dot(hidden_three, full_fc1, preferred_element_type=jnp.float32)
-    activated = gelu_tanh(pre_gelu).astype(jnp.bfloat16)
-    branch_three = jnp.dot(activated, full_fc2, preferred_element_type=jnp.float32)
-    layer_out = after_cross + modulation[8] * branch_three
-    upstream = out_grad[0].astype(jnp.float32)
-    dbranch_three = (modulation[8] * upstream).astype(jnp.bfloat16)
-    dgate_three = jnp.sum(upstream * branch_three, 0)
-    grad_fc2 = outer_sum(activated, dbranch_three)
-    dactivated = through(dbranch_three, full_fc2)
-    gelu_value, gelu_pull = jax.vjp(gelu_tanh, pre_gelu)
-    dinner = gelu_pull(dactivated)[0].astype(jnp.bfloat16)
-    grad_fc1 = outer_sum(hidden_three, dinner)
-    back_three, dshift_three, dscale_three = norm_back(
-        through(dinner, full_fc1), normed_three, inverse_three, modulation[7]
-    )
-    dcross = upstream + back_three
-    dbranch_two = (modulation[5] * dcross).astype(jnp.bfloat16)
-    dgate_two = jnp.sum(dcross * branch_two, 0)
-    grad_cout = outer_sum(mixed_two, dbranch_two)
-    dmixed_two = through(dbranch_two, full_cout).astype(jnp.bfloat16)
-    dquery_two, dkeys_two, dvalues_two = attend_back(
-        query_two, memory[:, 0], memory[:, 1], text_valid, log_two, dmixed_two
-    )
-    dquery_flat = dquery_two.astype(jnp.bfloat16)
-    dmemory = jnp.concatenate([dkeys_two, dvalues_two], -1).astype(jnp.bfloat16)
-    grad_cq = outer_sum(hidden_two, dquery_flat)
-    grad_ckv = outer_sum(text_block, dmemory)
-    text_grad = through(dmemory, full_ckv)
-    back_two, dshift_two, dscale_two = norm_back(
-        through(dquery_flat, full_cq), normed_two, inverse_two, modulation[4]
-    )
-    grad_self = dcross + back_two
-    dbranch_one = (modulation[2] * grad_self).astype(jnp.bfloat16)
-    dgate_one = jnp.sum(grad_self * branch_one, 0)
-    grad_out = outer_sum(mixed_one, dbranch_one)
-    dmixed_one = through(dbranch_one, full_out).astype(jnp.bfloat16)
-    dquery_one, dkeys_one, dvalues_one = attend_back(
-        packed[:, 0], packed[:, 1], packed[:, 2], frame_valid, log_one, dmixed_one
-    )
-    dpacked = jnp.concatenate([dquery_one, dkeys_one, dvalues_one], -1).astype(jnp.bfloat16)
-    grad_qkv = outer_sum(hidden_one, dpacked)
-    back_one, dshift_one, dscale_one = norm_back(
-        through(dpacked, full_qkv), normed_one, inverse_one, modulation[1]
-    )
-    latent_grad = grad_self + back_one
-    dmodulation = (
-        jnp.stack(
-            [
-                dshift_one,
-                dscale_one,
-                dgate_one,
-                dshift_two,
-                dscale_two,
-                dgate_two,
-                dshift_three,
-                dscale_three,
-                dgate_three,
-            ]
-        )
-        .reshape(1, -1)
-        .astype(jnp.bfloat16)
-    )
+    slot_count, model_width = latents.shape[1:]
+    text_slots = text_rows.shape[1]
+    padded = -(-slot_count // 128) * 128
+    frame_bias = jnp.where(jnp.arange(padded) < frame_len[0], 0.0, -1e30).astype(F32)[None]
+    text_bias = jnp.where(jnp.arange(text_slots) < text_len[0], 0.0, -1e30).astype(F32)[None]
+    modulation = jnp.pad(modulation, ((0, 7), (0, 0)))
+    results = forward(
+        latents[0], text_rows[0], out_grad[0], modulation, frame_bias, text_bias, matrices
+    )
+    layer_out = results[0]
+    kept = results[1:11]
+    grad_fc1, grad_fc2, rows_3 = results[11:]
+    results = backward(
+        latents[0], text_rows[0], modulation, frame_bias, text_bias, kept, matrices[:5]
+    )
+    latent_grad, text_grad, rows_1 = results[:3]
+    order = (
+        rows_1[3:4],
+        rows_1[4:5],
+        rows_1[2:3],
+        rows_1[0:1],
+        rows_1[1:2],
+        rows_3[3:4],
+        rows_3[1:2],
+        rows_3[2:3],
+        rows_3[0:1],
+    )
+    dmodulation = jnp.concatenate(order, 0).reshape(1, -1).astype(BF16)
     grad_ada = ada_gradient(grid, conditions, dmodulation)
-    owned = reduce_gradients(
-        grid, (grad_qkv, grad_out, grad_cq, grad_ckv, grad_cout, grad_fc1, grad_fc2)
-    )
-    owned_grads = (grad_ada, *owned)
+    owned = reduce_gradients(grid, (*results[3:8], grad_fc1, grad_fc2))
     return (
         layer_out[None],
         latent_grad[None],
         text_grad[None],
-        owned_grads[0],
-        owned_grads[1],
-        owned_grads[2],
-        owned_grads[3],
-        owned_grads[4],
-        owned_grads[5],
-        owned_grads[6],
-        owned_grads[7],
+        grad_ada,
+        *owned,
     )
 
 
 def solution(mesh):
-    placed = (
-        P(("dp", "fsdp"), None, None),
-        P(("dp", "fsdp"), None, None),
-        P(("dp", "fsdp"), None, None),
-        P(("dp", "fsdp")),
-        P(("dp", "fsdp")),
-        P(("dp", "fsdp")),
-        P("dp", "fsdp"),
-        P("dp", "fsdp"),
-        P("dp", "fsdp"),
-        P("dp", "fsdp"),
-        P("dp", "fsdp"),
-        P("dp", "fsdp"),
-        P("dp", "fsdp"),
-        P("dp", "fsdp"),
-    )
+    placed = (P(("dp", "fsdp"), None, None),) * 3 + (P(("dp", "fsdp")),) * 3 + (P("dp", "fsdp"),) * 8
     return jax.shard_map(
         functools.partial(body, dp_size=mesh.shape["dp"], fsdp_size=mesh.shape["fsdp"]),
         mesh=mesh,
         in_specs=placed,
-        out_specs=(
-            P(("dp", "fsdp"), None, None),
-            P(("dp", "fsdp"), None, None),
-            P(("dp", "fsdp"), None, None),
-            P("dp", "fsdp"),
-            P("dp", "fsdp"),
-            P("dp", "fsdp"),
-            P("dp", "fsdp"),
-            P("dp", "fsdp"),
-            P("dp", "fsdp"),
-            P("dp", "fsdp"),
-            P("dp", "fsdp"),
-        ),
+        out_specs=(P(("dp", "fsdp"), None, None),) * 3 + (P("dp", "fsdp"),) * 8,
         check_vma=False,
     )

time: 676 us -> 583 us (0.86)
  matrix products: 227 us -> 2.18 us
  Pallas kernels: 217 us -> 383 us
  waiting for transfers between devices: 3.14 us -> 59.7 us
  other arithmetic: 63.4 us -> 12.8 us
  local copies, waits for them, and re-layouts: 54.6 us -> 17.7 us
    dot_general x56 -> x0, matrix products: 186 us -> none  [the longest x7 39.5 us: through(): lax.dot_general(gradient, matrix, (((1,), (1,)), ((), ())), preferred_ele...]
    pallas_call x0 -> x2, Pallas kernels: none -> 166 us  [the longest x1 92.7 us: backward(): pl.pallas_call(backward_kernel, out_shape=outs, in_specs=[vmem] * 5 + [an...]
    unnamed x2, waiting for transfers between devices: 0.04 us -> 59.6 us
    dot_general x8 -> x1, matrix products: 38.5 us -> 1.22 us  [outer_sum(): lax.dot_general(left, right, (((0,), (0,)), ((), ())), preferred_element_...]
    convert_element_type x7 -> x1, other arithmetic: 23.3 us -> 0.73 us  [body(): dmodulation = jnp.concatenate(order, 0).reshape(1, -1).astype(BF16)]
    reduce_sum x11 -> x0, other arithmetic: 16.4 us -> none  [the longest x6 13 us: one_group(): summed = jnp.sum(exponent, -1, keepdims=True)]
    convert_element_type x6 -> x2, local copies, waits for them, and re-layouts: 13.6 us -> 0.61 us  [body(): dmodulation = jnp.concatenate(order, 0).reshape(1, -1).astype(BF16)]
    another operation x18 -> x0, local copies, waits for them, and re-layouts: 8.49 us -> none
  transfers between devices with their start and end apart: 17 -> 17, of which waited for: 1 -> 1; matrix products, arithmetic and copies ran while one was open for 5% -> 5% of each run, Pallas kernels for 32% -> 38%
where the time goes in v2:
time: 583 us; the launch traced here: 579 us
  Pallas kernels  383 us (66%)
  blocking collectives  74.5 us (13%)
  waiting for transfers between devices  59.7 us (10%)
  local copies, waits for them, and re-layouts  17.7 us (3%)
  between operations  17.2 us (3%)
  other arithmetic  12.8 us (2%)
  starting transfers between devices  11.2 us (2%)
    pallas_call x1, Pallas kernels, reduce_gradients(): pl.pallas_call(functools.partial(reduce_kernel, nz, count), out_shape=[ja...  116 us
    pallas_call x1, Pallas kernels, gather_weights(): pl.pallas_call(functools.partial(gather_kernel, nz, count), out_shape=sha...  101 us
    pallas_call x1, Pallas kernels, backward(): pl.pallas_call(backward_kernel, out_shape=outs, in_specs=[vmem] * 5 + [an...  92.7 us
    pallas_call x1, Pallas kernels, forward(): pl.pallas_call(forward_kernel, out_shape=outs, in_specs=[vmem] * 6 + [any...  73.3 us
    unnamed x2, waiting for transfers between devices  59.6 us
    unnamed x1, blocking collectives  41.5 us
    all_gather x1, blocking collectives, ada_gradient(): everyone = lax.all_gather(swapped, 'dp', axis=0, tiled=True)  33 us
  transfers between devices with their start and end apart: 17, of which 1 were waited for; matrix products, arithmetic and copies ran while one was open for 5% of the time, Pallas kernels for 38%

profile of v2, /device:TPU:0, one launch (start us, length us, event | category | flops | bytes accessed | tf_op | source)
XLA Modules:
  0.0 578.7 jit_solution(1464590235792313381)
XLA Ops:
  7.3 0.8 constant_dynamic-slice_fusion.25
  8.5 0.8 constant_dynamic-slice_fusion.23
  9.3 0.8 constant_dynamic-slice_fusion.19
  10.6 0.8 constant_dynamic-slice_fusion.21
  11.5 0.9 constant_dynamic-slice_fusion.27
  13.6 41.5 %all-reduce.1 = s32[32]{0:T(128)S(1)} all-reduce(s32[32]{0:T(128)S(1)} %dynamic-update-slice), channel_id=1, replica_groups=mesh['dp'=8,'fsdp'=4] {'dp','fsdp'}, use_global_device_ids=true, to_apply=%add.1 | all-reduce | flops 32 | bytes 256
  55.5 1.0 fusion.4
  57.8 0.6 compare_select_fusion.refs_4_.refs_3_
  58.3 0.9 constant_dynamic-slice_fusion.17
  59.3 1.1 constant_dynamic-slice_fusion.15
  61.2 0.6 dynamic-slice
  62.5 0.7 maximum_select_fusion.11.refs_1_
  63.7 0.7 maximum_select_fusion.12.refs_2_
  64.4 0.7 maximum_select_fusion.13.refs_4_
  65.1 0.7 maximum_select_fusion.10.refs_3_
  65.8 0.8 maximum_select_fusion.6.refs_0_
  66.6 0.7 maximum_select_fusion.3.refs_5_
  67.3 59.6 %all-reduce.5.cloned.1.call-done = f32[32,1728]{1,0:T(8,128)} async-done(((f32[32,1728]{1,0:T(8,128)}), f32[32,1728]{1,0:T(8,128)}) %all-reduce.5.cloned.1.call-update) | async-done | bytes 221200
  126.9 0.8 dynamic-slice_bitcast_fusion
  127.7 0.6 copy.33
  128.3 3.5 all-to-all-start
  131.8 0.8 maximum_select_fusion.4.refs_6_
  132.6 101.3 %gather_weights.1 = (bf16[4,2,2,48,2304]{4,3,2,1,0:T(8,128)(2,1)}, bf16[4,2,2,48,768]{4,3,2,1,0:T(8,128)(2,1)}, bf16[4,2,2,48,768]{4,3,2,1,0:T(8,128)(2,1)}, bf1...) custom-call(bf16[48,1152]{1,0:T(8,128)(2,1)} %maximum_select_fusion., ...), custom_call_target="tpu_custom_call" | custom-call | tf_op jit(solution)/shard_map/gather_weights/pallas_call | solution.py:203
  234.1 0.6 pad.4.refs_3_.refs_2_
  234.7 73.3 %forward.1 = (f32[864,768]{1,0:T(8,128)}, f32[864,768]{1,0:T(8,128)}, bf16[864,2304]{1,0:T(8,128)(2,1)}, bf16[864,768]{1,0:T(8,128)(2,1)}, bf16[864,768]{1,0:T(8...) custom-call(bf16[864,768]{1,0:T(8,128)(2,1)} %bitcast.17, ...), custom_call_target="tpu_custom_call" | custom-call | tf_op jit(solution)/shard_map/forward/pallas_call | solution.py:760
  308.0 0.7 convert.17
  308.8 92.7 %backward.1 = (f32[864,768]{1,0:T(8,128)}, f32[256,768]{1,0:T(8,128)}, f32[8,768]{1,0:T(8,128)}, bf16[4,2,2,48,2304]{4,3,2,1,0:T(8,128)(2,1)}, bf16[4,2,2,48,768...) custom-call(bf16[864,768]{1,0:T(8,128)(2,1)} %bitcast.18, ...), custom_call_target="tpu_custom_call" | custom-call | tf_op jit(solution)/shard_map/backward/pallas_call | solution.py:893
  401.5 0.7 convert.16
  402.9 0.7 reduce.1
  403.6 0.7 reshape.79
  404.3 3.5 all-to-all-start.1
  407.8 116.1 %reduce_gradients.1 = (f32[48,1152]{1,0:T(8,128)}, f32[48,384]{1,0:T(8,128)}, f32[48,384]{1,0:T(8,128)}, f32[48,768]{1,0:T(8,128)}, f32[48,384]{1,0:T(8,128)}, /*index=5*/f32[48,1536]{1,0:T(8,128)}, f32[192,384]{1,0:T(8,128)}) custom-call(bf16[4,2,2,48,2304]{4,3,2,1,0:T(8,128)(2,1)} %get-tuple-element.69.refs_0_, ...), custom_call_target="tpu_custom_call" | custom-call | tf_op jit(solution)/shard_map/reduce_gradients/pallas_call | solution.py:373
  523.9 1.0 constant_dynamic-slice_fusion.11
  525.0 1.0 constant_dynamic-slice_fusion.9
  526.0 0.6 collective-permute-start.9
  526.7 1.0 constant_dynamic-slice_fusion.5
  527.8 1.2 constant_dynamic-slice_fusion.1
  529.0 1.1 constant_dynamic-slice_fusion.13
  530.6 0.9 constant_dynamic-slice_fusion.7
  531.9 33.0 %all-gather = bf16[32,1,1728]{2,1,0:T(2,128)(2,1)S(1)} all-gather(bf16[4,1,1728]{2,1,0:T(2,128)(2,1)S(1)} %reshape.80), channel_id=2, replica_groups=mesh['dp'=8,'fsdp'=4] {'dp'}, dimensions={0}, use_global_device_ids=true | all-gather | bytes 124416 | tf_op jit(solution)/shard_map/all_gather | solution.py:420
  564.9 1.2 fusion
  566.1 0.7 maximum_select_fusion.7
  567.3 0.7 maximum_select_fusion.8
  567.9 0.7 maximum_select_fusion.9
  568.6 0.7 maximum_select_fusion.5
  569.3 0.7 maximum_select_fusion.2
  570.0 0.9 copy.37
  570.9 0.7 maximum_select_fusion.1
  (59 shorter events, 5.8 us)
Async XLA Ops:
  7.2 48.3 %copy-start = (bf16[96,1728]{1,0:T(8,128)(2,1)S(1)}, bf16[96,1728]{1,0:T(8,128)(2,1)}, u32[]{:S(2)}) copy-start(bf16[96,1728]{1,0:T(8,128)(2,1)} %param.20) | copy-start | bytes 995332
  7.2 54.0 %copy-start.3 = (u32[32]{0:T(128)S(1)}, u32[32]{0:T(128)}, u32[]{:S(2)}) copy-start(u32[32]{0:T(128)} %constant.69) | copy-start | bytes 388
  7.2 119.7 %all-reduce.5.cloned.1.call-start = ((), (), s32[]{:S(2)}) async-start(), calls=%async_computation.2 | async-start | bytes 458752
  8.1 54.4 %collective-permute-start.1 = (bf16[48,192]{1,0:T(8,128)(2,1)S(1)}, bf16[48,192]{1,0:T(8,128)(2,1)S(1)}, u32[]{:S(2)}, u32[]{:S(2)}) collective-permute-start(bf16[48,192]{1,0:T(8,128)(2,1)S(1)} %get-tuple-element.143), channel_id=1, source_target_pairs={{0,1},{1,0},{2,3},{3,2},{4,5},{5,4},{6,7},{7,6},{8,9},{9,8},{10,11... | collective-permute-start | bytes 55304 | tf_op jit(solution)/shard_map/ppermute | solution.py:78
  9.3 54.0 %collective-permute-start.2 = (bf16[48,192]{1,0:T(8,128)(2,1)S(1)}, bf16[48,192]{1,0:T(8,128)(2,1)S(1)}, u32[]{:S(2)}, u32[]{:S(2)}) collective-permute-start(bf16[48,192]{1,0:T(8,128)(2,1)S(1)} %get-tuple-element.141), channel_id=1, source_target_pairs={{0,1},{1,0},{2,3},{3,2},{4,5},{5,4},{6,7},{7,6},{8,9},{9,8},{10,11... | collective-permute-start | bytes 55304 | tf_op jit(solution)/shard_map/ppermute | solution.py:78
  10.1 54.3 %collective-permute-start.4 = (bf16[48,192]{1,0:T(8,128)(2,1)S(1)}, bf16[48,192]{1,0:T(8,128)(2,1)S(1)}, u32[]{:S(2)}, u32[]{:S(2)}) collective-permute-start(bf16[48,192]{1,0:T(8,128)(2,1)S(1)} %get-tuple-element.139), channel_id=1, source_target_pairs={{0,1},{1,0},{2,3},{3,2},{4,5},{5,4},{6,7},{7,6},{8,9},{9,8},{10,11... | collective-permute-start | bytes 55304 | tf_op jit(solution)/shard_map/ppermute | solution.py:78
  11.3 53.8 %collective-permute-start.3 = (bf16[48,384]{1,0:T(8,128)(2,1)S(1)}, bf16[48,384]{1,0:T(8,128)(2,1)S(1)}, u32[]{:S(2)}, u32[]{:S(2)}) collective-permute-start(bf16[48,384]{1,0:T(8,128)(2,1)S(1)} %get-tuple-element.137), channel_id=1, source_target_pairs={{0,1},{1,0},{2,3},{3,2},{4,5},{5,4},{6,7},{7,6},{8,9},{9,8},{10,11... | collective-permute-start | bytes 110600 | tf_op jit(solution)/shard_map/ppermute | solution.py:78
  12.3 53.5 %collective-permute-start = (bf16[48,576]{1,0:T(8,128)(2,1)S(1)}, bf16[48,576]{1,0:T(8,128)(2,1)S(1)}, u32[]{:S(2)}, u32[]{:S(2)}) collective-permute-start(bf16[48,576]{1,0:T(8,128)(2,1)S(1)} %get-tuple-element.129), channel_id=1, source_target_pairs={{0,1},{1,0},{2,3},{3,2},{4,5},{5,4},{6,7},{7,6},{8,9},{9,8},{10,11... | collective-permute-start | bytes 165896 | tf_op jit(solution)/shard_map/ppermute | solution.py:78
  62.5 4.1 collective-permute-start.5
  63.2 68.6 %collective-permute-start.6 = (bf16[192,192]{1,0:T(8,128)(2,1)S(1)}, bf16[192,192]{1,0:T(8,128)(2,1)S(1)}, u32[]{:S(2)}, u32[]{:S(2)}) collective-permute-start(bf16[192,192]{1,0:T(8,128)(2,1)S(1)} %copy.40), channel_id=1, source_target_pairs={{0,1},{1,0},{2,3},{3,2},{4,5},{5,4},{6,7},{7,6},{8,9},{9,8},{10,11... | collective-permute-start | bytes 221192 | tf_op jit(solution)/shard_map/ppermute | solution.py:78
  128.3 105.6 %all-to-all-start = ((f32[4,1,1728]{2,1,0:T(1,128)}), f32[4,1,1728]{2,1,0:T(1,128)S(1)}, u32[]{:S(2)}, u32[]{:S(2)}) async-start(f32[4,1,1728]{2,1,0:T(1,128)} %copy.33), calls=%async_computation | async-start | bytes 57344 | tf_op jit(solution)/shard_map/all_to_all | solution.py:413
  404.3 127.4 %all-to-all-start.1 = ((bf16[4,2,864]{2,1,0:T(2,128)(2,1)}), bf16[4,2,864]{2,1,0:T(2,128)(2,1)S(1)}, u32[]{:S(2)}, u32[]{:S(2)}) async-start(bf16[4,2,864]{2,1,0:T(2,128)(2,1)} %reshape.79), calls=%async_computation.1 | async-start | bytes 28672 | tf_op jit(solution)/shard_map/all_to_all | solution.py:419
  523.9 7.8 %copy-start.2 = (f32[48,1536]{1,0:T(8,128)S(1)}, f32[48,1536]{1,0:T(8,128)}, u32[]{:S(2)}) copy-start(f32[48,1536]{1,0:T(8,128)} %get-tuple-element.81) | copy-start | bytes 884740
  525.0 41.1 %collective-permute-start.8 = (f32[48,192]{1,0:T(8,128)S(1)}, f32[48,192]{1,0:T(8,128)S(1)}, u32[]{:S(2)}, u32[]{:S(2)}) collective-permute-start(f32[48,192]{1,0:T(8,128)S(1)} %get-tuple-element.135), channel_id=1, source_target_pairs={{0,1},{1,0},{2,3},{3,2},{4,5},{5,4},{6,7},{7,6},{8,9},{9,8},{10,11... | collective-permute-start | bytes 110600 | tf_op jit(solution)/shard_map/ppermute | solution.py:78
  526.0 40.7 %collective-permute-start.9 = (f32[48,192]{1,0:T(8,128)S(1)}, f32[48,192]{1,0:T(8,128)S(1)}, u32[]{:S(2)}, u32[]{:S(2)}) collective-permute-start(f32[48,192]{1,0:T(8,128)S(1)} %get-tuple-element.133), channel_id=1, source_target_pairs={{0,1},{1,0},{2,3},{3,2},{4,5},{5,4},{6,7},{7,6},{8,9},{9,8},{10,11... | collective-permute-start | bytes 110600 | tf_op jit(solution)/shard_map/ppermute | solution.py:78
  527.6 40.3 %collective-permute-start.11 = (f32[48,192]{1,0:T(8,128)S(1)}, f32[48,192]{1,0:T(8,128)S(1)}, u32[]{:S(2)}, u32[]{:S(2)}) collective-permute-start(f32[48,192]{1,0:T(8,128)S(1)} %get-tuple-element.131), channel_id=1, source_target_pairs={{0,1},{1,0},{2,3},{3,2},{4,5},{5,4},{6,7},{7,6},{8,9},{9,8},{10,11... | collective-permute-start | bytes 110600 | tf_op jit(solution)/shard_map/ppermute | solution.py:78
  530.2 39.1 %collective-permute-start.7 = (f32[48,576]{1,0:T(8,128)S(1)}, f32[48,576]{1,0:T(8,128)S(1)}, u32[]{:S(2)}, u32[]{:S(2)}) collective-permute-start(f32[48,576]{1,0:T(8,128)S(1)} %get-tuple-element.121), channel_id=1, source_target_pairs={{0,1},{1,0},{2,3},{3,2},{4,5},{5,4},{6,7},{7,6},{8,9},{9,8},{10,11... | collective-permute-start | bytes 331784 | tf_op jit(solution)/shard_map/ppermute | solution.py:78
  531.6 37.0 %collective-permute-start.10 = (f32[48,384]{1,0:T(8,128)S(1)}, f32[48,384]{1,0:T(8,128)S(1)}, u32[]{:S(2)}, u32[]{:S(2)}) collective-permute-start(f32[48,384]{1,0:T(8,128)S(1)} %get-tuple-element.123), channel_id=1, source_target_pairs={{0,1},{1,0},{2,3},{3,2},{4,5},{5,4},{6,7},{7,6},{8,9},{9,8},{10,11... | collective-permute-start | bytes 221192 | tf_op jit(solution)/shard_map/ppermute | solution.py:78
  531.7 39.9 %copy-start.1 = (bf16[96,1728]{1,0:T(8,128)(2,1)S(1)}, bf16[96,1728]{1,0:T(8,128)(2,1)}, u32[]{:S(2)}) copy-start(bf16[96,1728]{1,0:T(8,128)(2,1)} %param.20) | copy-start | bytes 995332
  566.1 3.9 collective-permute-start.13
  566.8 4.1 collective-permute-start.12
Sparse Core Ops, SparseCore 0:
  56.6 70.2 all-reduce.4
